TPU v7x, 32 devices: a whole 2x2x4 slice. The times are simulated.
32 devices in a mesh: role: 2 (over y), dp: 4 (over z), tp: 4 (over x, core).
Axes of the slice: x: 2, y: 2, z: 4, core: 2. Of those that a mesh axis runs over, the one named last changes fastest.
Arguments:
- hidden: bfloat16 [2, 512, 8192], P('role', 'dp'), may hold values from -6 to 6
- out_grad: bfloat16 [512, 1024], P('dp', 'tp'), may hold values from -6 to 6
- master: float32 [8192, 1024], P('dp', 'tp'), may hold values from -0.0625 to 0.0625
- moment1: float32 [8192, 1024], P('dp', 'tp'), may hold values from -18 to 18
- moment2: float32 [8192, 1024], P('dp', 'tp'), may hold values from 50 to 500
- queries: bfloat16 [8, 64, 8192], P(None, 'dp', 'tp'), may hold values from -160 to 160
- new_keys: bfloat16 [8, 64, 1024], P(None, 'dp', 'tp'), may hold values from -6 to 6
- k_cache: bfloat16 [64, 256, 1024], P('dp', None, 'tp'), may hold values from -6 to 6
- v_cache: bfloat16 [64, 256, 1024], P('dp', None, 'tp'), may hold values from -6 to 6
- cache_len: int32 [64], P('dp'), may hold values from 2 to 256, as said below
Outputs:
- row_result: bfloat16 [2, 512, 8192], P('role', 'dp', 'tp')
Inputs may be any that keep to these rules, and one draw needn't show every extreme that they name: `cache_len`: some row holds exactly 256 cached positions.
All inputs are finite; a program needn't handle non-finite values.
Results may differ from a plain program's by a relative error of at most 0.008.
Values may be sent and summed in bfloat16 or wider, within the bound.
A program may use at most 64 MiB of HBM per device.

v0:
```python
import jax
import jax.numpy as jnp
from jax import lax
from jax.sharding import PartitionSpec as P

D = 8192
KVH = 8
QH = 64
HD = 128
STEPS = 8


beta_one = 0.9
beta_two = 0.95
adam_eps = 1e-08
bias_one = 1.0 - 0.9**10
bias_two = 1.0 - 0.95**10
neg_fill = -1e30


def from_behind(value, axis, by):
    peers = lax.axis_size(axis)
    pairs = [(i, i + by) for i in range(peers) if 0 <= i + by < peers]
    return lax.ppermute(value, axis, pairs)


def adam_fresh(master, moment1, moment2, gradient):
    step_size = 2.0 * D ** (-0.5)
    first = beta_one * moment1 + (1.0 - beta_one) * gradient
    second = beta_two * moment2 + (1.0 - beta_two) * gradient * gradient
    change = first / bias_one / (jnp.sqrt(second / bias_two) + adam_eps)
    return (master - step_size * change).astype(jnp.bfloat16)


def stream_out(fresh):
    return from_behind(fresh, "role", 1)


def local(
    hidden, out_grad, master, moment1, moment2, queries, new_keys, k_cache, v_cache, cache_len
):
    group_index = lax.axis_index("role")
    is_learner = group_index == 0
    own_rows = hidden[0]
    width_here = out_grad.shape[1]
    heads_here = width_here // HD
    share = QH // KVH
    replica_rows = cache_len.shape[0]
    cache_size = k_cache.shape[1]
    columns = lax.all_to_all(own_rows, "dp", split_axis=1, concat_axis=0, tiled=True)
    picked = columns
    gradient = lax.dot_general(
        picked,
        lax.all_gather(out_grad, "dp", axis=0, tiled=True),
        (((0,), (0,)), ((), ())),
        preferred_element_type=jnp.float32,
    )
    fresh = adam_fresh(master, moment1, moment2, gradient)
    old_weight = master.astype(jnp.bfloat16)
    partial_value = lax.dot_general(
        out_grad,
        lax.all_gather(old_weight, "dp", axis=0, tiled=True),
        (((1,), (1,)), ((), ())),
        preferred_element_type=jnp.float32,
    )
    learner_rows = lax.psum_scatter(
        partial_value.astype(jnp.bfloat16), "tp", scatter_dimension=1, tiled=True
    )
    arrived = stream_out(fresh)
    picked = own_rows
    values = jnp.dot(
        picked,
        lax.all_gather(arrived, "dp", axis=0, tiled=True),
        preferred_element_type=jnp.float32,
    )
    values = values.astype(jnp.bfloat16).reshape(STEPS, replica_rows, heads_here, HD)
    query_all = queries.reshape(STEPS, replica_rows, heads_here, share, HD)
    newkey_all = new_keys.reshape(STEPS, replica_rows, heads_here, HD)
    cache_keys = k_cache.reshape(replica_rows, cache_size, heads_here, HD)
    cache_vals = v_cache.reshape(replica_rows, cache_size, heads_here, HD)
    scale = HD ** (-0.5)
    cache_score = (
        jnp.einsum("srkgd,rpkd->srkgp", query_all, cache_keys, preferred_element_type=jnp.float32)
        * scale
    )
    valid = jnp.arange(cache_size)[None, :] < cache_len[:, None]
    cache_score = jnp.where(valid[None, :, None, None, :], cache_score, neg_fill)
    fresh_score = (
        jnp.einsum("srkgd,trkd->srkgt", query_all, newkey_all, preferred_element_type=jnp.float32)
        * scale
    )
    causal = jnp.arange(STEPS)[:, None] >= jnp.arange(STEPS)[None, :]
    fresh_score = jnp.where(causal[:, None, None, None, :], fresh_score, neg_fill)
    top = jnp.maximum(jnp.max(cache_score, axis=-1), jnp.max(fresh_score, axis=-1))
    cache_exp = jnp.exp(cache_score - top[..., None])
    fresh_exp = jnp.exp(fresh_score - top[..., None])
    total = jnp.sum(cache_exp, axis=-1) + jnp.sum(fresh_exp, axis=-1)
    cache_wts = (cache_exp / total[..., None]).astype(jnp.bfloat16)
    fresh_wts = (fresh_exp / total[..., None]).astype(jnp.bfloat16)
    output = jnp.einsum(
        "srkgp,rpkd->srkgd", cache_wts, cache_vals, preferred_element_type=jnp.float32
    )
    output = output + jnp.einsum(
        "srkgt,trkd->srkgd", fresh_wts, values, preferred_element_type=jnp.float32
    )
    decoded = output.astype(jnp.bfloat16).reshape(STEPS * replica_rows, heads_here * share * HD)
    result = jnp.where(is_learner, learner_rows, decoded)
    return result[None]


def solution(mesh):
    return jax.shard_map(
        local,
        mesh=mesh,
        in_specs=(
            P("role", "dp", None),
            P("dp", "tp"),
            P("dp", "tp"),
            P("dp", "tp"),
            P("dp", "tp"),
            P(None, "dp", "tp"),
            P(None, "dp", "tp"),
            P("dp", None, "tp"),
            P("dp", None, "tp"),
            P("dp"),
        ),
        out_specs=P("role", "dp", "tp"),
        check_vma=False,
    )
```

profile of v0, /device:TPU:2, one launch (start us, length us, event | category | flops | bytes accessed | tf_op | source)
XLA Modules:
  0.0 283.7 jit_solution(4297813566451300308)
XLA Ops:
  6.5 4.1 %copy.33 = bf16[1,128,8192]{1,2,0:T(8,128)(2,1)} copy(bf16[1,128,8192]{2,1,0:T(8,128)(2,1)} %param.10) | data formatting | bytes 4194304 | tf_op args[0]
  10.6 5.0 %all-to-all-start = ((bf16[128,4,2048]{0,2,1:T(8,128)(2,1)}), bf16[128,4,2048]{0,2,1:T(8,128)(2,1)S(1)}, u32[]{:S(2)}, u32[]{:S(2)}) async-start(bf16[128,4,2048]{0,2,1:T(8,128)(2,1)} %bitcast.52), calls=%async_computation.1 | async-start | bytes 4194304 | tf_op jit(solution)/shard_map/all_to_all | solution.py:50
  15.6 55.9 %all_gather.10 = bf16[512,256]{1,0:T(8,128)(2,1)S(1)} all-gather(bf16[128,256]{1,0:T(8,128)(2,1)S(1)} %copy-done.7), channel_id=1, replica_groups=mesh['role'=2,'dp'=4,'tp'=4] {'dp'}, dimensions={0}, use_global_device_ids=true | all-gather | bytes 327680 | tf_op jit(solution)/shard_map/all_gather | solution.py:54
  71.5 2.6 copy.34
  74.2 7.3 %fusion.14 = (bf16[2048,256]{1,0:T(8,128)(2,1)S(1)}, bf16[2048,256]{1,0:T(8,128)(2,1)}) fusion(f32[2048,256]{1,0:T(8,128)} %param.12, f32[2048,256]{1,0:T(8,128)} %param.14, f32[2048,256]{1,0:T(8,128)} %param.13, bf16[512,2048]{1,0:T(8,128)(2,1)} %bitcast.57, bf16[512,256]{1,0:T(8,128)(2,1)S(1)} %all_gather.10), kind=kOutput, calls=%fused_computation.20 | convolution fusion | flops 544735232 | bytes 10747904 | tf_op jit(solution)/shard_map/dot_general | solution.py:52
  81.5 3.5 %collective-permute-start = (bf16[2048,256]{1,0:T(8,128)(2,1)S(1)}, bf16[2048,256]{1,0:T(8,128)(2,1)S(1)}, u32[]{:S(2)}, u32[]{:S(2)}) collective-permute-start(bf16[2048,256]{1,0:T(8,128)(2,1)S(1)} %get-tuple-element.5), channel_id=1, source_target_pairs={{0,16},{1,17},{2,18},{3,19},{4,20},{5,21},{6,22},{7,23},{8,24},{9,... | collective-permute-start | bytes 3145736 | tf_op jit(solution)/shard_map/ppermute | solution.py:24
  85.0 19.4 %collective-permute-done = bf16[2048,256]{1,0:T(8,128)(2,1)S(1)} collective-permute-done((bf16[2048,256]{1,0:T(8,128)(2,1)S(1)}, bf16[2048,256]{1,0:T(8,128)(2,1)S(1)}, u32[]{:S(2)}, u32[]{:S(2)}) %collective-permute-start) | collective-permute-done | bytes 1048608 | tf_op jit(solution)/shard_map/ppermute | solution.py:24
  104.4 1.0 copy-done.5
  105.5 57.5 %all-gather.3.cloned.1.call-done = bf16[8192,256]{1,0:T(8,128)(2,1)} async-done(((bf16[2048,256]{1,0:T(8,128)(2,1)}), bf16[8192,256]{1,0:T(8,128)(2,1)}) %all-gather.3.cloned.1.call-update) | async-done | bytes 4194320 | tf_op jit(solution)/shard_map/all_gather | solution.py:62
  163.0 5.1 %convolution_convert_fusion = bf16[128,8192]{1,0:T(8,128)(2,1)} fusion(bf16[128,256]{1,0:T(8,128)(2,1)S(1)} %copy-done.7, bf16[8192,256]{1,0:T(8,128)(2,1)} %all-gather.3.cloned.1.call-done), kind=kOutput, calls=%fused_computation | convolution fusion | flops 537919488 | bytes 6356992 | tf_op jit(solution)/shard_map/dot_general | solution.py:60
  168.2 0.1 copy.52
  168.3 0.7 copy-done.8
  169.0 0.8 copy-done.3
  169.7 2.1 reshape.61
  171.9 4.0 %reshape.64 = bf16[16,256,2,128]{3,2,1,0:T(2,128)(2,1)} reshape(bf16[16,256,256]{2,1,0:T(8,128)(2,1)} %param.18) | data formatting | bytes 4194304 | tf_op jit(solution)/shard_map/reshape | solution.py:80
  175.9 0.1 iota_compare_fusion
  175.9 2.4 fusion.47
  178.4 2.5 bitcast_reduce_fusion
  181.0 0.4 fusion.38
  181.4 0.9 copy-done.1
  182.3 0.9 fusion.15
  183.2 60.7 %all-gather.5.cloned.1.call-done = bf16[8192,256]{1,0:T(8,128)(2,1)} async-done(((bf16[2048,256]{1,0:T(8,128)(2,1)}), bf16[8192,256]{1,0:T(8,128)(2,1)}) %all-gather.5.cloned.1.call-update) | async-done | bytes 4194320 | tf_op jit(solution)/shard_map/all_gather | solution.py:73
  243.9 3.5 %fusion.30 = bf16[128,256]{0,1:T(8,128)(2,1)S(1)} fusion(bf16[8192,256]{1,0:T(8,128)(2,1)} %all-gather.5.cloned.1.call-done, bf16[1,128,8192]{2,1,0:T(8,128)(2,1)S(1)} %copy-done), kind=kOutput, calls=%fused_computation.30 | convolution fusion | flops 536903680 | bytes 6356992 | tf_op jit(solution)/shard_map/dot_general | solution.py:71
  247.4 0.1 copy.35
  247.6 0.5 convolution_bitcast_fusion
  248.0 1.1 copy-done.2
  249.1 0.6 copy-done.4
  249.8 1.1 fusion.24
  250.9 0.1 copy.38
  251.0 0.2 reshape.66
  251.2 24.1 %reduce-scatter.2.cloned.1.call-done = bf16[128,2048]{1,0:T(8,128)(2,1)} async-done(((bf16[128,8192]{1,0:T(8,128)(2,1)}), bf16[128,2048]{1,0:T(8,128)(2,1)}) %reduce-scatter.2.cloned.1.call-update) | async-done | bytes 524304 | tf_op jit(solution)/shard_map/reduce_scatter | solution.py:66
  275.2 1.9 select_bitcast_fusion
  (26 shorter events, 0.3 us)
Async XLA Ops:
  10.6 5.0 %copy-start.7 = (bf16[128,256]{1,0:T(8,128)(2,1)S(1)}, bf16[128,256]{1,0:T(8,128)(2,1)}, u32[]{:S(2)}) copy-start(bf16[128,256]{1,0:T(8,128)(2,1)} %param.11) | copy-start | bytes 196612
  10.6 60.9 %all-to-all-start = ((bf16[128,4,2048]{0,2,1:T(8,128)(2,1)}), bf16[128,4,2048]{0,2,1:T(8,128)(2,1)S(1)}, u32[]{:S(2)}, u32[]{:S(2)}) async-start(bf16[128,4,2048]{0,2,1:T(8,128)(2,1)} %bitcast.52), calls=%async_computation.1 | async-start | bytes 4194304 | tf_op jit(solution)/shard_map/all_to_all | solution.py:50
  15.6 147.4 %all-gather.3.cloned.1.call-start = ((), (), s32[]{:S(2)}) async-start(), calls=%async_computation.2 | async-start | bytes 5242880 | tf_op jit(solution)/shard_map/all_gather | solution.py:62
  81.5 162.4 %all-gather.5.cloned.1.call-start = ((), (), s32[]{:S(2)}) async-start(), calls=%async_computation.4 | async-start | bytes 5242880 | tf_op jit(solution)/shard_map/all_gather | solution.py:73
  81.5 22.9 %collective-permute-start = (bf16[2048,256]{1,0:T(8,128)(2,1)S(1)}, bf16[2048,256]{1,0:T(8,128)(2,1)S(1)}, u32[]{:S(2)}, u32[]{:S(2)}) collective-permute-start(bf16[2048,256]{1,0:T(8,128)(2,1)S(1)} %get-tuple-element.5), channel_id=1, source_target_pairs={{0,16},{1,17},{2,18},{3,19},{4,20},{5,21},{6,22},{7,23},{8,24},{9,... | collective-permute-start | bytes 3145736 | tf_op jit(solution)/shard_map/ppermute | solution.py:24
  104.4 1.0 copy-start.5
  105.4 169.8 %reduce-scatter.2.cloned.1.call-start = ((), (), s32[]{:S(2)}) async-start(), calls=%async_computation.3 | async-start | bytes 2621440 | tf_op jit(solution)/shard_map/reduce_scatter | solution.py:66
  163.0 5.1 %copy-start.6 = (bf16[8,16,2048]{2,1,0:T(8,128)(2,1)S(1)}, bf16[8,16,2048]{2,1,0:T(8,128)(2,1)}, u32[]{:S(2)}) copy-start(bf16[8,16,2048]{2,1,0:T(8,128)(2,1)} %param.15) | copy-start | bytes 1572868
  168.1 0.8 copy-start.8
  168.1 1.6 copy-start.3
  171.9 4.0 %copy-start.9 = (s32[16]{0:T(128)S(1)}, s32[16]{0:T(128)}, u32[]{:S(2)}) copy-start(s32[16]{0:T(128)} %param.19) | copy-start | bytes 196
  180.9 1.3 copy-start.1
  180.9 63.0 %copy-start = (bf16[1,128,8192]{2,1,0:T(8,128)(2,1)S(1)}, bf16[1,128,8192]{2,1,0:T(8,128)(2,1)}, u32[]{:S(2)}) copy-start(bf16[1,128,8192]{2,1,0:T(8,128)(2,1)} %param.10) | copy-start | bytes 6291460
  247.5 1.6 copy-start.2
  247.6 2.2 copy-start.4
Sparse Core Ops, SparseCore 0:
  81.6 81.3 all-gather.2
  164.6 79.2 all-gather.4
  246.5 28.7 reduce-scatter.1
where the time goes:
time: 287 us; the launch traced here: 284 us
  waiting for transfers between devices  162 us (56%)
  blocking collectives  55.9 us (19%)
  matrix products  22.3 us (8%)
  local copies, waits for them, and re-layouts  18.4 us (6%)
  between operations  13.3 us (5%)
  starting transfers between devices  8.57 us (3%)
  other arithmetic  3.37 us (1%)
    all_gather x1, waiting for transfers between devices, local(): lax.all_gather(arrived, 'dp', axis=0, tiled=True)  60.7 us
    all_gather x1, waiting for transfers between devices, local(): lax.all_gather(old_weight, 'dp', axis=0, tiled=True)  57.5 us
    all_gather x1, blocking collectives, local(): lax.all_gather(out_grad, 'dp', axis=0, tiled=True)  55.9 us
    reduce_scatter x1, waiting for transfers between devices, local(): lax.psum_scatter(partial_value.astype(jnp.bfloat16), 'tp', scatter_dimens...  24.1 us
    ppermute x1, waiting for transfers between devices, from_behind(): return lax.ppermute(value, axis, pairs)  19.4 us
    unnamed x22, local copies, waits for them, and re-layouts  9.23 us
    dot_general x1, matrix products, local(): lax.dot_general(picked, lax.all_gather(out_grad, 'dp', axis=0, tiled=True...  7.27 us
  transfers between devices with their start and end apart: 5, of which 4 were waited for; matrix products, arithmetic and copies ran while one was open for 8% of the time, Pallas kernels for 0%

commit v1 on v0

--- a/solution.py
+++ b/solution.py
@@ -1,6 +1,10 @@
+import functools
+
 import jax
 import jax.numpy as jnp
 from jax import lax
+from jax.experimental import pallas as pl
+from jax.experimental.pallas import tpu as pltpu
 from jax.sharding import PartitionSpec as P
 
 D = 8192
@@ -18,12 +22,6 @@
 neg_fill = -1e30
 
 
-def from_behind(value, axis, by):
-    peers = lax.axis_size(axis)
-    pairs = [(i, i + by) for i in range(peers) if 0 <= i + by < peers]
-    return lax.ppermute(value, axis, pairs)
-
-
 def adam_fresh(master, moment1, moment2, gradient):
     step_size = 2.0 * D ** (-0.5)
     first = beta_one * moment1 + (1.0 - beta_one) * gradient
@@ -32,8 +30,287 @@
     return (master - step_size * change).astype(jnp.bfloat16)
 
 
-def stream_out(fresh):
-    return from_behind(fresh, "role", 1)
+MESH = pl.DeviceIdType.MESH
+
+
+def position():
+    return lax.axis_index("role"), lax.axis_index("dp"), lax.axis_index("tp")
+
+
+def signal(semaphore, role, row, col):
+    pl.semaphore_signal(semaphore, inc=1, device_id=(role, row, col), device_id_type=MESH)
+
+
+def remote(src, dst, send, recv, role, row, col):
+    return pltpu.make_async_remote_copy(
+        src_ref=src,
+        dst_ref=dst,
+        send_sem=send,
+        recv_sem=recv,
+        device_id=(role, row, col),
+        device_id_type=MESH,
+    )
+
+
+def drain(ref, semaphore):
+    pltpu.make_async_copy(ref, ref, semaphore).wait()
+
+
+def each(count, body):
+    def step(k, carry):
+        body(k)
+        return carry
+
+    lax.fori_loop(0, count, step, 0)
+
+
+def spread_kernel(
+    n, m, hid, og, slabs, ogs,
+    og_send, og_recv, hid_send, hid_recv, loc, x_send, x_recv, c_send, c_recv,
+):
+    r, i, t = position()
+    rows, width = slabs.shape[3], slabs.shape[4]
+    pairs = m // 2
+    px, core = t // 2, t % 2
+
+    barrier = pltpu.get_barrier_semaphore()
+
+    def greet(k):
+        @pl.when(k != r * n + i)
+        def _():
+            signal(barrier, k // n, k % n, t)
+
+    def greet_tp(k):
+        @pl.when(k != t)
+        def _():
+            signal(barrier, r, i, k)
+
+    each(2 * n, greet)
+    each(m, greet_tp)
+    pl.semaphore_wait(barrier, 2 * n - 1 + m - 1)
+
+    def piece(j):
+        return hid.at[pl.ds(pl.multiple_of(t * rows, rows), rows), pl.ds(pl.multiple_of(j * width, width), width)]
+
+    def send_og(k):
+        j = (i + k) % n
+        remote(og, ogs.at[i], og_send, og_recv, r, j, t).start()
+
+    def send_hid(k):
+        j = (i + k) % n
+        remote(piece(j), slabs.at[r, t, i], hid_send, hid_recv.at[r], 1, j, t).start()
+
+    each(n - 1, lambda k: send_og(k + 1))
+    each(n - 1, lambda k: send_hid(k + 1))
+    og_local = pltpu.make_async_copy(og, ogs.at[i], loc.at[0])
+    og_local.start()
+
+    @pl.when(r == 0)
+    def _():
+        send_hid(0)
+
+    @pl.when(r == 1)
+    def _():
+        own = pltpu.make_async_copy(piece(i), slabs.at[1, t, i], loc.at[1])
+        own.start()
+
+        def to_pair(which, src):
+            return remote(
+                slabs.at[which, src * 2 + core],
+                slabs.at[which, src * 2 + core],
+                c_send.at[which, src],
+                c_recv.at[which, src],
+                1, i, t + 1 - 2 * core,
+            )
+
+        def from_pair(which, src):
+            drain(slabs.at[which, src * 2 + 1 - core], c_recv.at[which, src])
+
+        def over(which, step):
+            dst = (px + step) % pairs
+            return remote(
+                slabs.at[which, t],
+                slabs.at[which, t],
+                x_send.at[which, step],
+                x_recv.at[which, px],
+                1, i, dst * 2 + core,
+            )
+
+        for which in range(2):
+            if which == 0:
+                drain(slabs.at[0, t], hid_recv.at[0])
+            else:
+                drain(slabs.at[1, t, pl.ds(0, n - 1)], hid_recv.at[1])
+                own.wait()
+            for step in range(1, pairs):
+                over(which, step).start()
+            to_pair(which, px).start()
+        for which in range(2):
+            for step in range(1, pairs):
+                src = (px + step) % pairs
+                drain(slabs.at[which, src * 2 + core], x_recv.at[which, src])
+                to_pair(which, src).start()
+        for which in range(2):
+            for src in range(pairs):
+                from_pair(which, src)
+        for which in range(2):
+            for step in range(1, pairs):
+                over(which, step).wait_send()
+            for src in range(pairs):
+                to_pair(which, src).wait_send()
+        drain(slabs.at[1, t, pl.ds(0, n - 1)], hid_send)
+
+    @pl.when(r == 0)
+    def _():
+        drain(slabs.at[1, t], hid_send)
+
+    drain(ogs.at[pl.ds(0, n - 1)], og_send)
+    drain(ogs.at[pl.ds(0, n - 1)], og_recv)
+    og_local.wait()
+
+
+def spread(hid, og, n, m):
+    rows, width = hid.shape[0] // m, hid.shape[1] // n
+    dma = pltpu.SemaphoreType.DMA
+    anywhere = pl.BlockSpec(memory_space=pl.ANY)
+    return pl.pallas_call(
+        functools.partial(spread_kernel, n, m),
+        out_shape=(
+            jax.ShapeDtypeStruct((2, m, n, rows, width), hid.dtype),
+            jax.ShapeDtypeStruct((n,) + og.shape, og.dtype),
+        ),
+        in_specs=[anywhere] * 2,
+        out_specs=(anywhere, anywhere),
+        scratch_shapes=[
+            dma, dma, dma, dma((2,)), dma((2,)),
+            dma((2, m // 2)), dma((2, m // 2)), dma((2, m // 2)), dma((2, m // 2)),
+        ],
+        compiler_params=pltpu.CompilerParams(collective_id=0, has_side_effects=True),
+    )(hid, og)
+
+
+def total_of(slots, count, out, tile):
+    def chunk(k):
+        at = pl.ds(pl.multiple_of(k * tile, tile), tile)
+        total = slots[0, at, :].astype(jnp.float32)
+        for s in range(1, count):
+            total = total + slots[s, at, :].astype(jnp.float32)
+        out[at, :] = total.astype(out.dtype)
+
+    each(out.shape[0] // tile, chunk)
+
+
+def collect_kernel(
+    n, m, parts, sums, back, vals,
+    slots, reduced, val_slots, own_sem, p_send, p_recv, b_send, b_recv, v_send, v_recv,
+):
+    r, i, t = position()
+    q = n // m
+    width = parts.shape[2]
+    rows = back.shape[0]
+    home = i // q
+
+    barrier = pltpu.get_barrier_semaphore()
+
+    @pl.when(r == 0)
+    def _():
+        def greet_tp(k):
+            signal(barrier, 0, i, (t + 1 + k) % m)
+
+        def greet_far(k):
+            @pl.when(t * q + k != i)
+            def _():
+                signal(barrier, 0, t * q + k, home)
+
+        each(m - 1, greet_tp)
+        each(q, greet_far)
+        at_home = jnp.where(home == t, 1, 0)
+        pl.semaphore_wait(barrier, m - 1 + q - at_home)
+
+        def send_part(k):
+            g = (t + 1 + k) % m
+            remote(parts.at[g], slots.at[t], p_send, p_recv, 0, i, g).start()
+
+        each(m - 1, send_part)
+        mine = pltpu.make_async_copy(parts.at[t], slots.at[t], own_sem)
+        mine.start()
+        drain(slots.at[pl.ds(0, m - 1)], p_recv)
+        mine.wait()
+        total_of(slots, m, reduced, 16)
+
+        def place(j):
+            return back.at[:, pl.ds(pl.multiple_of((j % q) * width, width), width)]
+
+        def block(k):
+            return reduced.at[pl.ds(pl.multiple_of(k * rows, rows), rows)]
+
+        def send_block(k):
+            @pl.when(t * q + k != i)
+            def _():
+                remote(block(k), place(i), b_send, b_recv, 0, t * q + k, home).start()
+
+        each(q, send_block)
+
+        @pl.when(home == t)
+        def _():
+            keep = pltpu.make_async_copy(block(i % q), place(i), own_sem)
+            keep.start()
+            keep.wait()
+            if q > 1:
+                drain(reduced.at[pl.ds(0, (q - 1) * rows)], b_recv)
+                drain(reduced.at[pl.ds(0, (q - 1) * rows)], b_send)
+
+        @pl.when(home != t)
+        def _():
+            drain(reduced, b_recv)
+            drain(reduced, b_send)
+
+        drain(slots.at[pl.ds(0, m - 1)], p_send)
+
+    @pl.when(r == 1)
+    def _():
+        def greet_dp(k):
+            signal(barrier, 1, (i + 1 + k) % n, t)
+
+        each(n - 1, greet_dp)
+        pl.semaphore_wait(barrier, n - 1)
+
+        def send_sum(k):
+            j = (i + 1 + k) % n
+            remote(sums.at[j], val_slots.at[i], v_send, v_recv, 1, j, t).start()
+
+        each(n - 1, send_sum)
+        mine = pltpu.make_async_copy(sums.at[i], val_slots.at[i], own_sem)
+        mine.start()
+        drain(val_slots.at[pl.ds(0, n - 1)], v_recv)
+        mine.wait()
+        total_of(val_slots, n, vals, 16)
+        drain(val_slots.at[pl.ds(0, n - 1)], v_send)
+
+
+def collect(parts, sums, n, m):
+    q = n // m
+    rows, width = parts.shape[1] // q, parts.shape[2]
+    dma = pltpu.SemaphoreType.DMA
+    anywhere = pl.BlockSpec(memory_space=pl.ANY)
+    return pl.pallas_call(
+        functools.partial(collect_kernel, n, m),
+        out_shape=(
+            jax.ShapeDtypeStruct((rows, q * width), jnp.bfloat16),
+            jax.ShapeDtypeStruct(sums.shape[1:], jnp.bfloat16),
+        ),
+        in_specs=[anywhere] * 2,
+        out_specs=(anywhere, pl.BlockSpec(memory_space=pltpu.VMEM)),
+        scratch_shapes=[
+            pltpu.VMEM(parts.shape, jnp.bfloat16),
+            pltpu.VMEM(parts.shape[1:], jnp.bfloat16),
+            pltpu.VMEM(sums.shape, jnp.bfloat16),
+            dma, dma, dma, dma, dma, dma, dma,
+        ],
+        compiler_params=pltpu.CompilerParams(
+            collective_id=1, has_side_effects=True, vmem_limit_bytes=16 * 2**20
+        ),
+    )(parts, sums)
 
 
 def local(
@@ -47,33 +324,30 @@
     share = QH // KVH
     replica_rows = cache_len.shape[0]
     cache_size = k_cache.shape[1]
-    columns = lax.all_to_all(own_rows, "dp", split_axis=1, concat_axis=0, tiled=True)
-    picked = columns
+    n, m = lax.axis_size("dp"), lax.axis_size("tp")
+    slabs, ogs = spread(own_rows, out_grad, n, m)
+    rows, width = slabs.shape[3], slabs.shape[4]
+    grads = ogs.reshape(n, m, rows, width_here).transpose(1, 0, 2, 3)
     gradient = lax.dot_general(
-        picked,
-        lax.all_gather(out_grad, "dp", axis=0, tiled=True),
+        slabs[0].reshape(n * m * rows, width),
+        grads.reshape(n * m * rows, width_here),
         (((0,), (0,)), ((), ())),
         preferred_element_type=jnp.float32,
     )
     fresh = adam_fresh(master, moment1, moment2, gradient)
     old_weight = master.astype(jnp.bfloat16)
-    partial_value = lax.dot_general(
-        out_grad,
-        lax.all_gather(old_weight, "dp", axis=0, tiled=True),
+    parts = lax.dot_general(
+        ogs.reshape(n * m * rows, width_here),
+        old_weight,
         (((1,), (1,)), ((), ())),
         preferred_element_type=jnp.float32,
-    )
-    learner_rows = lax.psum_scatter(
-        partial_value.astype(jnp.bfloat16), "tp", scatter_dimension=1, tiled=True
-    )
-    arrived = stream_out(fresh)
-    picked = own_rows
-    values = jnp.dot(
-        picked,
-        lax.all_gather(arrived, "dp", axis=0, tiled=True),
-        preferred_element_type=jnp.float32,
-    )
-    values = values.astype(jnp.bfloat16).reshape(STEPS, replica_rows, heads_here, HD)
+    ).astype(jnp.bfloat16)
+    sums = jnp.dot(
+        slabs[1].reshape(n * m * rows, width), fresh, preferred_element_type=jnp.float32
+    ).astype(jnp.bfloat16)
+    sums = sums.reshape(m, n, rows, width_here).transpose(1, 0, 2, 3).reshape(n, m * rows, width_here)
+    learner_rows, values = collect(parts.reshape(m, n * rows, width), sums, n, m)
+    values = values.reshape(STEPS, replica_rows, heads_here, HD)
     query_all = queries.reshape(STEPS, replica_rows, heads_here, share, HD)
     newkey_all = new_keys.reshape(STEPS, replica_rows, heads_here, HD)
     cache_keys = k_cache.reshape(replica_rows, cache_size, heads_here, HD)

time: 287 us -> 98.3 us (0.34)
  the two profiles are of different devices: /device:TPU:2 before, /device:TPU:25 now
where the time goes in v1:
time: 98.3 us; the launch traced here: 98 us
  Pallas kernels  65 us (66%)
  matrix products  19.1 us (19%)
  local copies, waits for them, and re-layouts  11.4 us (12%)
  other arithmetic  2.33 us (2%)
    pallas_call x1, Pallas kernels, collect(): pl.pallas_call(functools.partial(collect_kernel, n, m), out_shape=(jax.Sh...  49.3 us
    pallas_call x1, Pallas kernels, spread(): pl.pallas_call(functools.partial(spread_kernel, n, m), out_shape=(jax.Sha...  15.7 us
    dot_general x1, matrix products, local(): jnp.dot(slabs[1].reshape(n * m * rows, width), fresh, preferred_element_t...  7.38 us
    reshape x1, local copies, waits for them, and re-layouts, local(): cache_vals = v_cache.reshape(replica_rows, cache_size, heads_here, HD)  4.11 us
    reshape x1, local copies, waits for them, and re-layouts, local(): cache_keys = k_cache.reshape(replica_rows, cache_size, heads_here, HD)  3.96 us
    dot_general x1, matrix products, local(): jnp.einsum('srkgp,rpkd->srkgd', cache_wts, cache_vals, preferred_element_...  2.75 us
    dot_general x1, matrix products, local(): lax.dot_general(ogs.reshape(n * m * rows, width_here), old_weight, (((1,)...  2.56 us
    dot_general x1, matrix products, local(): jnp.einsum('srkgd,rpkd->srkgp', query_all, cache_keys, preferred_element_...  2.51 us

profile of v1, /device:TPU:25, one launch (start us, length us, event | category | flops | bytes accessed | tf_op | source)
XLA Modules:
  0.0 98.0 jit_solution(10657648827925497505)
XLA Ops:
  0.0 15.7 %shard_map.100 = (bf16[2,4,4,32,2048]{4,3,2,1,0:T(8,128)(2,1)}, bf16[4,128,256]{2,1,0:T(8,128)(2,1)}) custom-call(bf16[128,8192]{1,0:T(8,128)(2,1)} %bitcast.55, bf16[128,256]{1,0:T(8,128)(2,1)} %og.1), custom_call_target="tpu_custom_call" | custom-call | tf_op jit(solution)/shard_map/pallas_call | solution.py:176
  15.7 0.0 copy-start
  15.7 2.6 %convolution_convert_fusion = bf16[512,2048]{1,0:T(8,128)(2,1)S(1)} fusion(bf16[512,256]{1,0:T(8,128)(2,1)} %bitcast.60, f32[2048,256]{1,0:T(8,128)} %param.12), kind=kOutput, calls=%fused_computation.1 | convolution fusion | flops 538443776 | bytes 4456448 | tf_op jit(solution)/shard_map/dot_general | solution.py:339
  18.3 0.3 copy-done
  18.6 0.0 copy-start.3
  18.6 2.5 %fusion.49 = (bf16[1,4,4,32,2048]{4,3,2,1,0:T(8,128)(2,1)}, bf16[1,4,4,32,2048]{4,3,2,1,0:T(8,128)(2,1)}) fusion(bf16[2,4,4,32,2048]{4,3,2,1,0:T(8,128)(2,1)S(1)} %copy-done), kind=kLoop, calls=%fused_computation.56 | loop fusion | bytes 8388608 | tf_op jit(solution)/shard_map/slice | solution.py:332
  21.1 0.0 copy-done.3
  21.1 7.4 %convolution_convert_fusion.1 = bf16[512,256]{1,0:T(8,128)(2,1)S(1)} fusion(bf16[512,2048]{1,0:T(8,128)(2,1)} %bitcast.59, f32[2048,256]{1,0:T(8,128)} %param.12, f32[2048,256]{1,0:T(8,128)} %param.14, f32[2048,256]{1,0:T(8,128)} %param.13, bf16[512,2048]{1,0:T(8,128)(2,1)} %bitcast.58, bf16[512,256]{1,0:T(8,128)(2,1)S(1)} %bitcast.64), kind=kOutput, calls=%fused_computation.27 | convolution fusion | flops 1081212928 | bytes 11010048 | tf_op jit(solution)/shard_map/dot_general | solution.py:345
  28.5 0.0 copy-start.4
  28.5 0.0 copy-start.5
  28.5 0.0 copy-start.6
  28.6 49.3 %shard_map.101 = (bf16[128,2048]{1,0:T(8,128)(2,1)S(1)}, bf16[128,256]{1,0:T(8,128)(2,1)S(1)}) custom-call(bf16[4,128,2048]{2,1,0:T(8,128)(2,1)S(1)} %bitcast.51, bf16[4,128,256]{2,1,0:T(8,128)(2,1)S(1)} %bitcast.52), custom_call_target="tpu_custom_call" | custom-call | tf_op jit(solution)/shard_map/pallas_call | solution.py:296
  77.9 0.0 copy-done.4
  77.9 0.1 copy.43
  78.0 0.0 copy-done.5
  78.1 2.4 %fusion.50 = (f32[8,16,2,8]{3,0,2,1:T(8,128)S(1)}, f32[8,16,2,8,8]{3,4,0,2,1:T(8,128)S(1)}) fusion(bf16[8,16,2,8,128]{4,3,2,1,0:T(8,128)(2,1)S(1)} %bitcast.53, bf16[8,16,2,128,1]{3,2,1,0,4:T(2,128)(2,1)S(1)} %bitcast.63, pred[8,8]{1,0:T(8,128)(4,1)S(1)} %iota_compare_fusion.1), kind=kOutput, calls=%fused_computation.57 | convolution fusion | flops 4241408 | bytes 663616 | tf_op jit(solution)/shard_map/srkgd,trkd->srkgt/dot_general | solution.py:363
  80.5 0.0 copy-done.6
  80.5 0.1 iota_compare_fusion
  80.6 4.0 %reshape.81 = bf16[16,256,2,128]{3,2,1,0:T(2,128)(2,1)} reshape(bf16[16,256,256]{2,1,0:T(8,128)(2,1)} %param.17) | data formatting | bytes 4194304 | tf_op jit(solution)/shard_map/reshape | solution.py:353
  84.6 2.5 %bitcast_reduce_fusion = (f32[8,16,2,8]{3,0,2,1:T(8,128)S(1)}, f32[16,2,256,8,8]{2,4,3,1,0:T(8,128)S(1)}) fusion(pred[16,256]{1,0:T(8,128)(4,1)S(1)} %iota_compare_fusion, bf16[8,16,2,8,128]{4,3,2,1,0:T(8,128)(2,1)S(1)} %bitcast.54, bf16[16,256,2,128,1]{3,2,1,0,4:T(2,128)(2,1)} %bitcast.57), kind=kOutput, calls=%fused_computation.12 | convolution fusion | flops 135788544 | bytes 4730880 | tf_op jit(solution)/shard_map/srkgd,rpkd->srkgp/dot_general | solution.py:357
  87.1 0.0 copy-start.1
  87.1 0.9 fusion.13
  88.0 0.4 fusion.32
  88.5 0.0 copy-done.1
  88.5 1.4 %convolution_bitcast_fusion = f32[8,16,2,8,128]{4,3,0,2,1:T(8,128)} fusion(f32[8,16,2,8,8]{3,4,0,2,1:T(8,128)S(1)} %get-tuple-element.18, f32[8,16,2,8]{3,0,2,1:T(8,128)S(1)} %add.26, f32[8,16,2,8]{3,0,2,1:T(8,128)S(1)} %max.7, bf16[8,16,2,128,1]{3,2,1,0,4:T(2,128)(2,1)S(1)} %bitcast.66), kind=kOutput, calls=%fused_computation.20 | convolution fusion | flops 4243456 | bytes 1196032 | tf_op jit(solution)/shard_map/srkgt,trkd->srkgd/dot_general | solution.py:377
  90.0 0.0 copy-start.2
  90.0 4.1 %reshape.84 = bf16[16,256,2,128]{3,2,1,0:T(2,128)(2,1)} reshape(bf16[16,256,256]{2,1,0:T(8,128)(2,1)} %param.18) | data formatting | bytes 4194304 | tf_op jit(solution)/shard_map/reshape | solution.py:354
  94.1 0.0 copy-done.2
  94.1 2.8 %fusion.22 = bf16[8,16,2,8,128]{4,3,0,2,1:T(8,128)(2,1)S(1)} fusion(f32[8,16,2,8,128]{4,3,0,2,1:T(8,128)} %convolution_bitcast_fusion, bf16[16,256,2,128,1]{3,2,1,0,4:T(2,128)(2,1)} %bitcast.56, f32[16,2,256,8,8]{2,4,3,1,0:T(8,128)S(1)} %copy-done.2, f32[8,16,2,8]{3,0,2,1:T(8,128)S(1)} %add.26, f32[8,16,2,8]{3,0,2,1:T(8,128)S(1)} %max.7, ...), kind=kOutput, calls=%fused_computation.26 | convolution fusion | flops 137363456 | bytes 5787648 | tf_op jit(solution)/shard_map/srkgp,rpkd->srkgd/dot_general | solution.py:374
  96.9 0.1 copy.29
  97.0 0.2 reshape.86
  97.2 0.9 select_bitcast_fusion
  (7 shorter events, 0.1 us)
Async XLA Ops:
  15.7 2.9 %copy-start = (bf16[2,4,4,32,2048]{4,3,2,1,0:T(8,128)(2,1)S(1)}, bf16[2,4,4,32,2048]{4,3,2,1,0:T(8,128)(2,1)}, u32[]{:S(2)}) copy-start(bf16[2,4,4,32,2048]{4,3,2,1,0:T(8,128)(2,1)} %get-tuple-element.10) | copy-start | bytes 12582916
  18.6 2.5 %copy-start.3 = (bf16[4,128,256]{2,1,0:T(8,128)(2,1)S(1)}, bf16[4,128,256]{2,1,0:T(8,128)(2,1)}, u32[]{:S(2)}) copy-start(bf16[4,128,256]{2,1,0:T(8,128)(2,1)} %get-tuple-element.9) | copy-start | bytes 786436
  28.5 49.4 %copy-start.4 = (bf16[8,16,2048]{2,1,0:T(8,128)(2,1)S(1)}, bf16[8,16,2048]{2,1,0:T(8,128)(2,1)}, u32[]{:S(2)}) copy-start(bf16[8,16,2048]{2,1,0:T(8,128)(2,1)} %param.15) | copy-start | bytes 1572868
  28.5 49.5 %copy-start.5 = (bf16[8,16,256]{2,1,0:T(8,128)(2,1)S(1)}, bf16[8,16,256]{2,1,0:T(8,128)(2,1)}, u32[]{:S(2)}) copy-start(bf16[8,16,256]{2,1,0:T(8,128)(2,1)} %param.16) | copy-start | bytes 196612
  28.5 52.0 %copy-start.6 = (s32[16]{0:T(128)S(1)}, s32[16]{0:T(128)}, u32[]{:S(2)}) copy-start(s32[16]{0:T(128)} %param.19) | copy-start | bytes 196
  87.1 1.4 %copy-start.1 = (f32[16,2,256,8,8]{2,4,3,1,0:T(8,128)}, f32[16,2,256,8,8]{2,4,3,1,0:T(8,128)S(1)}, u32[]{:S(2)}) copy-start(f32[16,2,256,8,8]{2,4,3,1,0:T(8,128)S(1)} %get-tuple-element.16) | copy-start | bytes 6291460
  90.0 4.1 %copy-start.2 = (f32[16,2,256,8,8]{2,4,3,1,0:T(8,128)S(1)}, f32[16,2,256,8,8]{2,4,3,1,0:T(8,128)}, u32[]{:S(2)}) copy-start(f32[16,2,256,8,8]{2,4,3,1,0:T(8,128)} %copy-done.1) | copy-start | bytes 6291460

commit v2 on v1

--- a/solution.py
+++ b/solution.py
@@ -65,7 +65,7 @@
 
 
 def spread_kernel(
-    n, m, hid, og, slabs, ogs,
+    n, m, split, hid, og, slabs, ogs,
     og_send, og_recv, hid_send, hid_recv, loc, x_send, x_recv, c_send, c_recv,
 ):
     r, i, t = position()
@@ -89,29 +89,34 @@
     each(m, greet_tp)
     pl.semaphore_wait(barrier, 2 * n - 1 + m - 1)
 
-    def piece(j):
-        return hid.at[pl.ds(pl.multiple_of(t * rows, rows), rows), pl.ds(pl.multiple_of(j * width, width), width)]
+    full = hid.shape[1] // n
+
+    def piece(role, j):
+        start = j * full + (role * width if split else 0)
+        return hid.at[pl.ds(pl.multiple_of(t * rows, rows), rows), pl.ds(pl.multiple_of(start, width), width)]
 
     def send_og(k):
         j = (i + k) % n
         remote(og, ogs.at[i], og_send, og_recv, r, j, t).start()
 
-    def send_hid(k):
-        j = (i + k) % n
-        remote(piece(j), slabs.at[r, t, i], hid_send, hid_recv.at[r], 1, j, t).start()
+    def send_hid(role, j):
+        remote(piece(role, j), slabs.at[r, t, i], hid_send.at[role], hid_recv.at[r], role, j, t).start()
 
     each(n - 1, lambda k: send_og(k + 1))
-    each(n - 1, lambda k: send_hid(k + 1))
+    targets = (0, 1) if split else (1,)
+    for role in targets:
+        each(n - 1, lambda k, role=role: send_hid(role, (i + k + 1) % n))
+
+        @pl.when(r != role)
+        def _(role=role):
+            send_hid(role, i)
+
     og_local = pltpu.make_async_copy(og, ogs.at[i], loc.at[0])
     og_local.start()
 
-    @pl.when(r == 0)
+    @pl.when((r == 1) | split)
     def _():
-        send_hid(0)
-
-    @pl.when(r == 1)
-    def _():
-        own = pltpu.make_async_copy(piece(i), slabs.at[1, t, i], loc.at[1])
+        own = pltpu.make_async_copy(piece(r, i), slabs.at[r, t, i], loc.at[1])
         own.start()
 
         def to_pair(which, src):
@@ -120,7 +125,7 @@
                 slabs.at[which, src * 2 + core],
                 c_send.at[which, src],
                 c_recv.at[which, src],
-                1, i, t + 1 - 2 * core,
+                r, i, t + 1 - 2 * core,
             )
 
         def from_pair(which, src):
@@ -133,15 +138,19 @@
                 slabs.at[which, t],
                 x_send.at[which, step],
                 x_recv.at[which, px],
-                1, i, dst * 2 + core,
+                r, i, dst * 2 + core,
             )
 
         for which in range(2):
-            if which == 0:
-                drain(slabs.at[0, t], hid_recv.at[0])
-            else:
-                drain(slabs.at[1, t, pl.ds(0, n - 1)], hid_recv.at[1])
+            @pl.when(r != which)
+            def _(which=which):
+                drain(slabs.at[which, t], hid_recv.at[which])
+
+            @pl.when(r == which)
+            def _(which=which):
+                drain(slabs.at[which, t, pl.ds(0, n - 1)], hid_recv.at[which])
                 own.wait()
+
             for step in range(1, pairs):
                 over(which, step).start()
             to_pair(which, px).start()
@@ -158,23 +167,27 @@
                 over(which, step).wait_send()
             for src in range(pairs):
                 to_pair(which, src).wait_send()
-        drain(slabs.at[1, t, pl.ds(0, n - 1)], hid_send)
-
-    @pl.when(r == 0)
-    def _():
-        drain(slabs.at[1, t], hid_send)
+
+    for role in targets:
+        @pl.when(r != role)
+        def _(role=role):
+            drain(slabs.at[role, t], hid_send.at[role])
+
+        @pl.when(r == role)
+        def _(role=role):
+            drain(slabs.at[role, t, pl.ds(0, n - 1)], hid_send.at[role])
 
     drain(ogs.at[pl.ds(0, n - 1)], og_send)
     drain(ogs.at[pl.ds(0, n - 1)], og_recv)
     og_local.wait()
 
 
-def spread(hid, og, n, m):
-    rows, width = hid.shape[0] // m, hid.shape[1] // n
+def spread(hid, og, n, m, split):
+    rows, width = hid.shape[0] // m, hid.shape[1] // n // (2 if split else 1)
     dma = pltpu.SemaphoreType.DMA
     anywhere = pl.BlockSpec(memory_space=pl.ANY)
     return pl.pallas_call(
-        functools.partial(spread_kernel, n, m),
+        functools.partial(spread_kernel, n, m, split),
         out_shape=(
             jax.ShapeDtypeStruct((2, m, n, rows, width), hid.dtype),
             jax.ShapeDtypeStruct((n,) + og.shape, og.dtype),
@@ -182,7 +195,7 @@
         in_specs=[anywhere] * 2,
         out_specs=(anywhere, anywhere),
         scratch_shapes=[
-            dma, dma, dma, dma((2,)), dma((2,)),
+            dma, dma, dma((2,)), dma((2,)), dma((2,)),
             dma((2, m // 2)), dma((2, m // 2)), dma((2, m // 2)), dma((2, m // 2)),
         ],
         compiler_params=pltpu.CompilerParams(collective_id=0, has_side_effects=True),
@@ -201,14 +214,32 @@
 
 
 def collect_kernel(
-    n, m, parts, sums, back, vals,
-    slots, reduced, val_slots, own_sem, p_send, p_recv, b_send, b_recv, v_send, v_recv,
+    n, m, split, ogs, master, sums, back, vals,
+    parts, slots, reduced, val_slots, own_sem, p_send, p_recv, b_send, b_recv, v_send, v_recv,
 ):
     r, i, t = position()
     q = n // m
     width = parts.shape[2]
     rows = back.shape[0]
     home = i // q
+    chunk = min(512, width)
+    sources = val_slots.shape[0]
+
+    def send_sum(j):
+        slot = r * n + i if split else i
+        remote(sums.at[j], val_slots.at[slot], v_send, v_recv, 1, j, t).start()
+
+    def fill_part(g):
+        def columns(k):
+            at = pl.ds(pl.multiple_of(k * chunk, chunk), chunk)
+            parts[g, :, at] = lax.dot_general(
+                ogs[g],
+                master[at, :].astype(jnp.bfloat16),
+                (((1,), (1,)), ((), ())),
+                preferred_element_type=jnp.float32,
+            ).astype(jnp.bfloat16)
+
+        each(width // chunk, columns)
 
     barrier = pltpu.get_barrier_semaphore()
 
@@ -225,13 +256,17 @@
         each(m - 1, greet_tp)
         each(q, greet_far)
         at_home = jnp.where(home == t, 1, 0)
-        pl.semaphore_wait(barrier, m - 1 + q - at_home)
+        pl.semaphore_wait(barrier, m - 1 + q - at_home + (n if split else 0))
+        if split:
+            each(n, lambda k: send_sum((i + k) % n))
 
         def send_part(k):
             g = (t + 1 + k) % m
+            fill_part(g)
             remote(parts.at[g], slots.at[t], p_send, p_recv, 0, i, g).start()
 
         each(m - 1, send_part)
+        fill_part(t)
         mine = pltpu.make_async_copy(parts.at[t], slots.at[t], own_sem)
         mine.start()
         drain(slots.at[pl.ds(0, m - 1)], p_recv)
@@ -266,6 +301,8 @@
             drain(reduced, b_send)
 
         drain(slots.at[pl.ds(0, m - 1)], p_send)
+        if split:
+            drain(val_slots.at[pl.ds(0, n)], v_send)
 
     @pl.when(r == 1)
     def _():
@@ -273,44 +310,44 @@
             signal(barrier, 1, (i + 1 + k) % n, t)
 
         each(n - 1, greet_dp)
+        if split:
+            each(n, lambda k: signal(barrier, 0, k, t))
         pl.semaphore_wait(barrier, n - 1)
-
-        def send_sum(k):
-            j = (i + 1 + k) % n
-            remote(sums.at[j], val_slots.at[i], v_send, v_recv, 1, j, t).start()
-
-        each(n - 1, send_sum)
-        mine = pltpu.make_async_copy(sums.at[i], val_slots.at[i], own_sem)
+        each(n - 1, lambda k: send_sum((i + 1 + k) % n))
+        mine = pltpu.make_async_copy(sums.at[i], val_slots.at[n + i if split else i], own_sem)
         mine.start()
-        drain(val_slots.at[pl.ds(0, n - 1)], v_recv)
+        drain(val_slots.at[pl.ds(0, sources - 1)], v_recv)
         mine.wait()
-        total_of(val_slots, n, vals, 16)
+        total_of(val_slots, sources, vals, 16)
         drain(val_slots.at[pl.ds(0, n - 1)], v_send)
 
 
-def collect(parts, sums, n, m):
+def collect(ogs, master, sums, n, m, split):
     q = n // m
-    rows, width = parts.shape[1] // q, parts.shape[2]
+    rows, width = ogs.shape[1] // q, master.shape[0]
+    parts = pltpu.VMEM((m, q * rows, width), jnp.bfloat16)
     dma = pltpu.SemaphoreType.DMA
     anywhere = pl.BlockSpec(memory_space=pl.ANY)
+    inside = pl.BlockSpec(memory_space=pltpu.VMEM)
     return pl.pallas_call(
-        functools.partial(collect_kernel, n, m),
+        functools.partial(collect_kernel, n, m, split),
         out_shape=(
             jax.ShapeDtypeStruct((rows, q * width), jnp.bfloat16),
             jax.ShapeDtypeStruct(sums.shape[1:], jnp.bfloat16),
         ),
-        in_specs=[anywhere] * 2,
-        out_specs=(anywhere, pl.BlockSpec(memory_space=pltpu.VMEM)),
+        in_specs=[inside, inside, anywhere],
+        out_specs=(anywhere, inside),
         scratch_shapes=[
-            pltpu.VMEM(parts.shape, jnp.bfloat16),
-            pltpu.VMEM(parts.shape[1:], jnp.bfloat16),
-            pltpu.VMEM(sums.shape, jnp.bfloat16),
+            parts,
+            parts,
+            pltpu.VMEM((q * rows, width), jnp.bfloat16),
+            pltpu.VMEM((n * (2 if split else 1),) + sums.shape[1:], jnp.bfloat16),
             dma, dma, dma, dma, dma, dma, dma,
         ],
         compiler_params=pltpu.CompilerParams(
-            collective_id=1, has_side_effects=True, vmem_limit_bytes=16 * 2**20
+            collective_id=1, has_side_effects=True, vmem_limit_bytes=32 * 2**20
         ),
-    )(parts, sums)
+    )(ogs, master, sums)
 
 
 def local(
@@ -320,12 +357,9 @@
     is_learner = group_index == 0
     own_rows = hidden[0]
     width_here = out_grad.shape[1]
-    heads_here = width_here // HD
-    share = QH // KVH
-    replica_rows = cache_len.shape[0]
-    cache_size = k_cache.shape[1]
     n, m = lax.axis_size("dp"), lax.axis_size("tp")
-    slabs, ogs = spread(own_rows, out_grad, n, m)
+    split = (own_rows.shape[1] // n) % 256 == 0
+    slabs, ogs = spread(own_rows, out_grad, n, m, split)
     rows, width = slabs.shape[3], slabs.shape[4]
     grads = ogs.reshape(n, m, rows, width_here).transpose(1, 0, 2, 3)
     gradient = lax.dot_general(
@@ -334,19 +368,31 @@
         (((0,), (0,)), ((), ())),
         preferred_element_type=jnp.float32,
     )
-    fresh = adam_fresh(master, moment1, moment2, gradient)
-    old_weight = master.astype(jnp.bfloat16)
-    parts = lax.dot_general(
-        ogs.reshape(n * m * rows, width_here),
-        old_weight,
-        (((1,), (1,)), ((), ())),
-        preferred_element_type=jnp.float32,
-    ).astype(jnp.bfloat16)
+    first_row = group_index * width if split else 0
+    mine = [
+        lax.dynamic_slice_in_dim(a, first_row, width, axis=0) for a in (master, moment1, moment2)
+    ]
+    fresh = adam_fresh(*mine, gradient)
     sums = jnp.dot(
         slabs[1].reshape(n * m * rows, width), fresh, preferred_element_type=jnp.float32
     ).astype(jnp.bfloat16)
     sums = sums.reshape(m, n, rows, width_here).transpose(1, 0, 2, 3).reshape(n, m * rows, width_here)
-    learner_rows, values = collect(parts.reshape(m, n * rows, width), sums, n, m)
+    learner_rows, values = collect(
+        ogs.reshape(m, n * rows, width_here), master, sums, n, m, split
+    )
+    result = lax.cond(
+        is_learner,
+        lambda: learner_rows,
+        lambda: attend(values, queries, new_keys, k_cache, v_cache, cache_len),
+    )
+    return result[None]
+
+
+def attend(values, queries, new_keys, k_cache, v_cache, cache_len):
+    heads_here = values.shape[1] // HD
+    share = QH // KVH
+    replica_rows = cache_len.shape[0]
+    cache_size = k_cache.shape[1]
     values = values.reshape(STEPS, replica_rows, heads_here, HD)
     query_all = queries.reshape(STEPS, replica_rows, heads_here, share, HD)
     newkey_all = new_keys.reshape(STEPS, replica_rows, heads_here, HD)
@@ -377,9 +423,7 @@
     output = output + jnp.einsum(
         "srkgt,trkd->srkgd", fresh_wts, values, preferred_element_type=jnp.float32
     )
-    decoded = output.astype(jnp.bfloat16).reshape(STEPS * replica_rows, heads_here * share * HD)
-    result = jnp.where(is_learner, learner_rows, decoded)
-    return result[None]
+    return output.astype(jnp.bfloat16).reshape(STEPS * replica_rows, heads_here * share * HD)
 
 
 def solution(mesh):

time: 98.3 us -> 94.5 us (0.961)
  the two profiles are of different devices: /device:TPU:25 before, /device:TPU:24 now
where the time goes in v2:
time: 94.5 us; the launch traced here: 94.2 us
  Pallas kernels  84.2 us (89%)
  local copies, waits for them, and re-layouts  5.51 us (6%)
  matrix products  4.41 us (5%)
    pallas_call x1, Pallas kernels, collect(): pl.pallas_call(functools.partial(collect_kernel, n, m, split), out_shape=...  53.4 us
    pallas_call x1, Pallas kernels, spread(): pl.pallas_call(functools.partial(spread_kernel, n, m, split), out_shape=(...  30.8 us
    dot_general x1, matrix products, local(): jnp.dot(slabs[1].reshape(n * m * rows, width), fresh, preferred_element_t...  4.41 us
    slice x1, local copies, waits for them, and re-layouts, local(): slabs[0].reshape(n * m * rows, width)  2.94 us

profile of v2, /device:TPU:24, one launch (start us, length us, event | category | flops | bytes accessed | tf_op | source)
XLA Modules:
  0.0 94.2 jit_solution(10927151263301964609)
XLA Ops:
  0.0 30.8 %shard_map.107 = (bf16[2,4,4,32,1024]{4,3,2,1,0:T(8,128)(2,1)}, bf16[4,128,256]{2,1,0:T(8,128)(2,1)}) custom-call(bf16[128,8192]{1,0:T(8,128)(2,1)} %bitcast.45, bf16[128,256]{1,0:T(8,128)(2,1)} %og.1), custom_call_target="tpu_custom_call" | custom-call | tf_op jit(solution)/shard_map/pallas_call | solution.py:189
  30.8 0.0 copy-start.1
  30.8 0.0 copy-start
  30.8 2.9 %fusion.49 = (bf16[1,4,4,32,1024]{4,3,2,1,0:T(8,128)(2,1)S(1)}, bf16[1,4,4,32,1024]{4,3,2,1,0:T(8,128)(2,1)}) fusion(bf16[2,4,4,32,1024]{4,3,2,1,0:T(8,128)(2,1)} %get-tuple-element.34), kind=kLoop, calls=%fused_computation.53 | loop fusion | bytes 4194304 | tf_op jit(solution)/shard_map/slice | solution.py:366
  33.8 0.0 copy-done.1
  33.8 0.7 copy.34
  34.5 0.0 copy-done
  34.5 4.4 %convolution_convert_fusion = bf16[512,256]{1,0:T(8,128)(2,1)} fusion(bf16[512,1024]{1,0:T(8,128)(2,1)} %bitcast.49, f32[2048,256]{1,0:T(8,128)} %param.16, s32[]{:T(128)S(6)} %select_n.16, f32[2048,256]{1,0:T(8,128)} %param.15, f32[2048,256]{1,0:T(8,128)S(1)} %copy-done, bf16[512,1024]{1,0:T(8,128)(2,1)S(1)} %bitcast.48, bf16[512,256]{1,0:T(8,128)(2,1)} %bitcast.54), kind=kOutput, calls=%fused_computation.34 | convolution fusion | flops 540672000 | bytes 5767172 | tf_op jit(solution)/shard_map/dot_general | solution.py:376
  38.9 0.0 copy-start.4
  38.9 0.0 copy-start.5
  38.9 0.0 copy-start.6
  38.9 1.0 %copy.35 = bf16[4,4,32,256]{3,2,0,1:T(8,128)(2,1)S(1)} copy(bf16[4,4,32,256]{3,2,1,0:T(8,128)(2,1)} %bitcast.53) | data formatting | bytes 524288 | tf_op jit(solution)/shard_map/reshape | solution.py:379
  39.9 53.4 %shard_map.108 = (bf16[128,2048]{1,0:T(8,128)(2,1)S(1)}, bf16[128,256]{1,0:T(8,128)(2,1)S(1)}) custom-call(bf16[4,128,256]{2,1,0:T(8,128)(2,1)S(1)} %copy-done.1, f32[2048,256]{1,0:T(8,128)S(1)} %copy-done, bf16[4,128,256]{2,1,0:T(8,128)(2,1)S(1)} %bitcast.42), custom_call_target="tpu_custom_call" | custom-call | tf_op jit(solution)/shard_map/pallas_call | solution.py:332
  93.4 0.0 copy-done.4
  93.4 0.0 copy-done.5
  93.4 0.0 copy-done.6
  93.4 0.8 copy.79
  (1 shorter events, 0.0 us)
Async XLA Ops:
  30.8 3.0 %copy-start.1 = (bf16[4,128,256]{2,1,0:T(8,128)(2,1)S(1)}, bf16[4,128,256]{2,1,0:T(8,128)(2,1)}, u32[]{:S(2)}) copy-start(bf16[4,128,256]{2,1,0:T(8,128)(2,1)} %get-tuple-element.33.ogs) | copy-start | bytes 786436
  30.8 3.7 %copy-start = (f32[2048,256]{1,0:T(8,128)S(1)}, f32[2048,256]{1,0:T(8,128)}, u32[]{:S(2)}) copy-start(f32[2048,256]{1,0:T(8,128)} %master.1) | copy-start | bytes 6291460
  38.9 54.5 %copy-start.4 = (bf16[8,16,2048]{2,1,0:T(8,128)(2,1)S(1)}, bf16[8,16,2048]{2,1,0:T(8,128)(2,1)}, u32[]{:S(2)}) copy-start(bf16[8,16,2048]{2,1,0:T(8,128)(2,1)} %param.17) | copy-start | bytes 1572868
  38.9 54.5 %copy-start.5 = (bf16[8,16,256]{2,1,0:T(8,128)(2,1)S(1)}, bf16[8,16,256]{2,1,0:T(8,128)(2,1)}, u32[]{:S(2)}) copy-start(bf16[8,16,256]{2,1,0:T(8,128)(2,1)} %param.18) | copy-start | bytes 196612
  38.9 54.5 %copy-start.6 = (s32[16]{0:T(128)S(1)}, s32[16]{0:T(128)}, u32[]{:S(2)}) copy-start(s32[16]{0:T(128)} %param.21) | copy-start | bytes 196

commit v3 on v0

v3 whole, which is shorter than its diff:
```python
import functools

import jax
import jax.numpy as jnp
from jax import lax
from jax.experimental import pallas as pl
from jax.experimental.pallas import tpu as pltpu
from jax.sharding import PartitionSpec as P

D = 8192
KVH = 8
QH = 64
HD = 128
STEPS = 8


beta_one = 0.9
beta_two = 0.95
adam_eps = 1e-08
bias_one = 1.0 - 0.9**10
bias_two = 1.0 - 0.95**10
neg_fill = -1e30


def adam_fresh(master, moment1, moment2, gradient):
    step_size = 2.0 * D ** (-0.5)
    first = beta_one * moment1 + (1.0 - beta_one) * gradient
    second = beta_two * moment2 + (1.0 - beta_two) * gradient * gradient
    change = first / bias_one / (jnp.sqrt(second / bias_two) + adam_eps)
    return (master - step_size * change).astype(jnp.bfloat16)


MESH = pl.DeviceIdType.MESH


def position():
    return lax.axis_index("role"), lax.axis_index("dp"), lax.axis_index("tp")


def signal(semaphore, role, row, col):
    pl.semaphore_signal(semaphore, inc=1, device_id=(role, row, col), device_id_type=MESH)


def remote(src, dst, send, recv, role, row, col):
    return pltpu.make_async_remote_copy(
        src_ref=src,
        dst_ref=dst,
        send_sem=send,
        recv_sem=recv,
        device_id=(role, row, col),
        device_id_type=MESH,
    )


def drain(ref, semaphore):
    pltpu.make_async_copy(ref, ref, semaphore).wait()


def each(count, body):
    def step(k, carry):
        body(k)
        return carry

    lax.fori_loop(0, count, step, 0)


def total_of(slots, count, out, tile):
    def chunk(k):
        at = pl.ds(pl.multiple_of(k * tile, tile), tile)
        total = slots[0, at, :].astype(jnp.float32)
        for s in range(1, count):
            total = total + slots[s, at, :].astype(jnp.float32)
        out[at, :] = total.astype(out.dtype)

    each(out.shape[0] // tile, chunk)


def fused_kernel(
    n, m, split, hid, og, master, moment1, moment2, back, vals,
    slabs, ogs, master_v, moment1_v, moment2_v, fresh, sums, parts, slots, reduced, val_slots,
    og_send, og_recv, hid_send, hid_recv, loc, x_send, x_recv, c_send, c_recv,
    p_send, p_recv, b_send, b_recv, v_send, v_recv,
):
    r, i, t = position()
    q = n // m
    rows, width = slabs.shape[3], slabs.shape[4]
    full = master.shape[0]
    heads = og.shape[1]
    home = i // q
    pairs = m // 2
    px, core = t // 2, t % 2
    sources = val_slots.shape[0]
    active = (r == 1) | split

    loads = [pltpu.make_async_copy(master, master_v, loc.at[2])]
    first = pl.multiple_of((r * width) if split else 0, width)
    for k, (src, dst) in enumerate(((moment1, moment1_v), (moment2, moment2_v))):
        loads.append(pltpu.make_async_copy(src.at[pl.ds(first, width)], dst, loc.at[3 + k]))
    for load in loads:
        load.start()

    barrier = pltpu.get_barrier_semaphore()

    def greet(k):
        @pl.when(k != r * n + i)
        def _():
            signal(barrier, k // n, k % n, t)

    def greet_tp(k):
        signal(barrier, r, i, (t + 1 + k) % m)

    def greet_far(k):
        @pl.when(t * q + k != i)
        def _():
            signal(barrier, 0, t * q + k, home)

    each(2 * n, greet)
    each(m - 1, greet_tp)

    @pl.when(r == 0)
    def _():
        each(q, greet_far)
        pl.semaphore_wait(barrier, 2 * n - 1 + m - 1 + q - jnp.where(home == t, 1, 0))

    @pl.when(r == 1)
    def _():
        pl.semaphore_wait(barrier, 2 * n - 1 + m - 1)

    def piece(role, j):
        start = j * full + (role * width if split else 0)
        return hid.at[pl.ds(pl.multiple_of(t * rows, rows), rows), pl.ds(pl.multiple_of(start, width), width)]

    def send_og(k):
        j = (i + k) % n
        remote(og, ogs.at[i], og_send, og_recv, r, j, t).start()

    def send_hid(role, j):
        remote(piece(role, j), slabs.at[r, t, i], hid_send.at[role], hid_recv.at[r], role, j, t).start()

    each(n - 1, lambda k: send_og(k + 1))
    targets = (0, 1) if split else (1,)
    for role in targets:
        each(n - 1, lambda k, role=role: send_hid(role, (i + k + 1) % n))

        @pl.when(r != role)
        def _(role=role):
            send_hid(role, i)

    og_local = pltpu.make_async_copy(og, ogs.at[i], loc.at[0])
    og_local.start()

    def to_pair(which, src):
        return remote(
            slabs.at[which, src * 2 + core],
            slabs.at[which, src * 2 + core],
            c_send.at[which, src],
            c_recv.at[which, src],
            r, i, t + 1 - 2 * core,
        )

    def from_pair(which, src):
        drain(slabs.at[which, src * 2 + 1 - core], c_recv.at[which, src])

    def over(which, step):
        dst = (px + step) % pairs
        return remote(
            slabs.at[which, t],
            slabs.at[which, t],
            x_send.at[which, step],
            x_recv.at[which, px],
            r, i, dst * 2 + core,
        )

    @pl.when(active)
    def _():
        own = pltpu.make_async_copy(piece(r, i), slabs.at[r, t, i], loc.at[1])
        own.start()
        for which in range(2):
            @pl.when(r != which)
            def _(which=which):
                drain(slabs.at[which, t], hid_recv.at[which])

            @pl.when(r == which)
            def _(which=which):
                drain(slabs.at[which, t, pl.ds(0, n - 1)], hid_recv.at[which])
                own.wait()

            for step in range(1, pairs):
                over(which, step).start()
            to_pair(which, px).start()

    drain(ogs.at[pl.ds(0, n - 1)], og_recv)
    og_local.wait()
    for load in loads:
        load.wait()

    chunk = min(512, full)
    block_rows = q * og.shape[0]

    def fill_part(g):
        tokens = ogs[pl.ds(g * q, q)].reshape(block_rows, heads)

        def columns(k):
            at = pl.ds(pl.multiple_of(k * chunk, chunk), chunk)
            parts[g, :, at] = lax.dot_general(
                tokens,
                master_v[at, :].astype(jnp.bfloat16),
                (((1,), (1,)), ((), ())),
                preferred_element_type=jnp.float32,
            ).astype(jnp.bfloat16)

        each(full // chunk, columns)

    mine = pltpu.make_async_copy(parts.at[t], slots.at[t], loc.at[0])

    @pl.when(r == 0)
    def _():
        def send_part(k):
            g = (t + 1 + k) % m
            fill_part(g)
            remote(parts.at[g], slots.at[t], p_send, p_recv, 0, i, g).start()

        each(m - 1, send_part)
        fill_part(t)
        mine.start()

    def send_sum(j):
        slot = r * n + i if split else i
        remote(sums.at[j], val_slots.at[slot], v_send, v_recv, 1, j, t).start()

    @pl.when(active)
    def _():
        for which in range(2):
            for step in range(1, pairs):
                src = (px + step) % pairs
                drain(slabs.at[which, src * 2 + core], x_recv.at[which, src])
                to_pair(which, src).start()
        for src in range(pairs):
            from_pair(0, src)

        tile = min(256, width)

        def update(k):
            at = pl.ds(pl.multiple_of(k * tile, tile), tile)
            gradient = jnp.zeros((tile, heads), jnp.float32)
            for g in range(m):
                gradient = gradient + lax.dot_general(
                    slabs[0, g, :, :, at].reshape(n * rows, tile),
                    ogs[:, g * rows : (g + 1) * rows, :].reshape(n * rows, heads),
                    (((0,), (0,)), ((), ())),
                    preferred_element_type=jnp.float32,
                )
            held = pl.ds(pl.multiple_of(first + k * tile, tile), tile)
            fresh[at, :] = adam_fresh(master_v[held, :], moment1_v[at, :], moment2_v[at, :], gradient)

        each(width // tile, update)
        for src in range(pairs):
            from_pair(1, src)
        for g in range(m):
            sums[:, g * rows : (g + 1) * rows, :] = (
                jnp.dot(
                    slabs[1, g].reshape(n * rows, width), fresh[...], preferred_element_type=jnp.float32
                )
                .astype(jnp.bfloat16)
                .reshape(n, rows, heads)
            )
        each(n - 1, lambda k: send_sum((i + 1 + k) % n))

        @pl.when(r == 0)
        def _():
            send_sum(i)

    @pl.when(r == 0)
    def _():
        drain(slots.at[pl.ds(0, m - 1)], p_recv)
        mine.wait()
        total_of(slots, m, reduced, 16)
        size = back.shape[0]

        def place(j):
            return back.at[:, pl.ds(pl.multiple_of((j % q) * full, full), full)]

        def block(k):
            return reduced.at[pl.ds(pl.multiple_of(k * size, size), size)]

        def send_block(k):
            @pl.when(t * q + k != i)
            def _():
                remote(block(k), place(i), b_send, b_recv, 0, t * q + k, home).start()

        each(q, send_block)

        @pl.when(home == t)
        def _():
            keep = pltpu.make_async_copy(block(i % q), place(i), loc.at[0])
            keep.start()
            keep.wait()
            if q > 1:
                drain(reduced.at[pl.ds(0, (q - 1) * size)], b_recv)
                drain(reduced.at[pl.ds(0, (q - 1) * size)], b_send)

        @pl.when(home != t)
        def _():
            drain(reduced, b_recv)
            drain(reduced, b_send)

        drain(slots.at[pl.ds(0, m - 1)], p_send)
        if split:
            drain(val_slots.at[pl.ds(0, n)], v_send)

    @pl.when(r == 1)
    def _():
        kept = pltpu.make_async_copy(sums.at[i], val_slots.at[n + i if split else i], loc.at[0])
        kept.start()
        drain(val_slots.at[pl.ds(0, sources - 1)], v_recv)
        kept.wait()
        total_of(val_slots, sources, vals, 16)
        drain(val_slots.at[pl.ds(0, n - 1)], v_send)

    @pl.when(active)
    def _():
        for which in range(2):
            for step in range(1, pairs):
                over(which, step).wait_send()
            for src in range(pairs):
                to_pair(which, src).wait_send()

    for role in targets:
        @pl.when(r != role)
        def _(role=role):
            drain(slabs.at[role, t], hid_send.at[role])

        @pl.when(r == role)
        def _(role=role):
            drain(slabs.at[role, t, pl.ds(0, n - 1)], hid_send.at[role])

    drain(ogs.at[pl.ds(0, n - 1)], og_send)


def fused(hid, og, master, moment1, moment2, n, m):
    q = n // m
    full, heads = master.shape
    tokens = og.shape[0]
    split = full % 256 == 0
    width = full // 2 if split else full
    dma = pltpu.SemaphoreType.DMA
    anywhere = pl.BlockSpec(memory_space=pl.ANY)
    half = pltpu.VMEM((width, heads), jnp.float32)
    block = pltpu.VMEM((m, q * tokens, full), jnp.bfloat16)
    return pl.pallas_call(
        functools.partial(fused_kernel, n, m, split),
        out_shape=(
            jax.ShapeDtypeStruct((tokens, q * full), jnp.bfloat16),
            jax.ShapeDtypeStruct((tokens, heads), jnp.bfloat16),
        ),
        in_specs=[anywhere] * 5,
        out_specs=(anywhere, pl.BlockSpec(memory_space=pltpu.VMEM)),
        scratch_shapes=[
            pltpu.VMEM((2, m, n, tokens // m, width), jnp.bfloat16),
            pltpu.VMEM((n, tokens, heads), jnp.bfloat16),
            pltpu.VMEM((full, heads), jnp.float32),
            half,
            half,
            pltpu.VMEM((width, heads), jnp.bfloat16),
            pltpu.VMEM((n, tokens, heads), jnp.bfloat16),
            block,
            block,
            pltpu.VMEM((q * tokens, full), jnp.bfloat16),
            pltpu.VMEM((n * (2 if split else 1), tokens, heads), jnp.bfloat16),
            dma, dma, dma((2,)), dma((2,)), dma((5,)),
            dma((2, m // 2)), dma((2, m // 2)), dma((2, m // 2)), dma((2, m // 2)),
            dma, dma, dma, dma, dma, dma,
        ],
        compiler_params=pltpu.CompilerParams(
            collective_id=0, has_side_effects=True, vmem_limit_bytes=40 * 2**20
        ),
    )(hid, og, master, moment1, moment2)


def local(
    hidden, out_grad, master, moment1, moment2, queries, new_keys, k_cache, v_cache, cache_len
):
    is_learner = lax.axis_index("role") == 0
    n, m = lax.axis_size("dp"), lax.axis_size("tp")
    learner_rows, values = fused(hidden[0], out_grad, master, moment1, moment2, n, m)
    result = lax.cond(
        is_learner,
        lambda: learner_rows,
        lambda: attend(values, queries, new_keys, k_cache, v_cache, cache_len),
    )
    return result[None]


def attend(values, queries, new_keys, k_cache, v_cache, cache_len):
    heads_here = values.shape[1] // HD
    share = QH // KVH
    replica_rows = cache_len.shape[0]
    cache_size = k_cache.shape[1]
    values = values.reshape(STEPS, replica_rows, heads_here, HD)
    query_all = queries.reshape(STEPS, replica_rows, heads_here, share, HD)
    newkey_all = new_keys.reshape(STEPS, replica_rows, heads_here, HD)
    cache_keys = k_cache.reshape(replica_rows, cache_size, heads_here, HD)
    cache_vals = v_cache.reshape(replica_rows, cache_size, heads_here, HD)
    scale = HD ** (-0.5)
    cache_score = (
        jnp.einsum("srkgd,rpkd->srkgp", query_all, cache_keys, preferred_element_type=jnp.float32)
        * scale
    )
    valid = jnp.arange(cache_size)[None, :] < cache_len[:, None]
    cache_score = jnp.where(valid[None, :, None, None, :], cache_score, neg_fill)
    fresh_score = (
        jnp.einsum("srkgd,trkd->srkgt", query_all, newkey_all, preferred_element_type=jnp.float32)
        * scale
    )
    causal = jnp.arange(STEPS)[:, None] >= jnp.arange(STEPS)[None, :]
    fresh_score = jnp.where(causal[:, None, None, None, :], fresh_score, neg_fill)
    top = jnp.maximum(jnp.max(cache_score, axis=-1), jnp.max(fresh_score, axis=-1))
    cache_exp = jnp.exp(cache_score - top[..., None])
    fresh_exp = jnp.exp(fresh_score - top[..., None])
    total = jnp.sum(cache_exp, axis=-1) + jnp.sum(fresh_exp, axis=-1)
    cache_wts = (cache_exp / total[..., None]).astype(jnp.bfloat16)
    fresh_wts = (fresh_exp / total[..., None]).astype(jnp.bfloat16)
    output = jnp.einsum(
        "srkgp,rpkd->srkgd", cache_wts, cache_vals, preferred_element_type=jnp.float32
    )
    output = output + jnp.einsum(
        "srkgt,trkd->srkgd", fresh_wts, values, preferred_element_type=jnp.float32
    )
    return output.astype(jnp.bfloat16).reshape(STEPS * replica_rows, heads_here * share * HD)


def solution(mesh):
    return jax.shard_map(
        local,
        mesh=mesh,
        in_specs=(
            P("role", "dp", None),
            P("dp", "tp"),
            P("dp", "tp"),
            P("dp", "tp"),
            P("dp", "tp"),
            P(None, "dp", "tp"),
            P(None, "dp", "tp"),
            P("dp", None, "tp"),
            P("dp", None, "tp"),
            P("dp"),
        ),
        out_specs=P("role", "dp", "tp"),
        check_vma=False,
    )
```

time: 287 us -> 78.2 us (0.27)
  the two profiles are of different devices: /device:TPU:2 before, /device:TPU:25 now
where the time goes in v3:
time: 78.2 us; the launch traced here: 77.8 us
  Pallas kernels  69.7 us (89%)
  local copies, waits for them, and re-layouts  8.01 us (10%)
    pallas_call x1, Pallas kernels, fused(): pl.pallas_call(functools.partial(fused_kernel, n, m, split), out_shape=(j...  69.7 us
    unnamed x17, local copies, waits for them, and re-layouts  8.01 us

profile of v3, /device:TPU:25, one launch (start us, length us, event | category | flops | bytes accessed | tf_op | source)
XLA Modules:
  0.0 77.8 jit_solution(15162688503878378714)
XLA Ops:
  0.0 0.0 copy-start
  0.0 1.6 %copy-done = bf16[1,128,8192]{2,1,0:T(8,128)(2,1)S(1)} copy-done((bf16[1,128,8192]{2,1,0:T(8,128)(2,1)S(1)}, bf16[1,128,8192]{2,1,0:T(8,128)(2,1)}, u32[]{:S(2)}) %copy-start) | copy-done | bytes 2097176
  1.6 0.0 copy-start.1
  1.6 1.6 %copy-done.1 = f32[2048,256]{1,0:T(8,128)S(1)} copy-done((f32[2048,256]{1,0:T(8,128)S(1)}, f32[2048,256]{1,0:T(8,128)}, u32[]{:S(2)}) %copy-start.1) | copy-done | bytes 2097176
  3.2 0.0 copy-start.2
  3.2 1.6 %copy-done.2 = f32[2048,256]{1,0:T(8,128)S(1)} copy-done((f32[2048,256]{1,0:T(8,128)S(1)}, f32[2048,256]{1,0:T(8,128)}, u32[]{:S(2)}) %copy-start.2) | copy-done | bytes 2097176
  4.8 0.0 copy-start.3
  4.8 1.6 %copy-done.3 = f32[2048,256]{1,0:T(8,128)S(1)} copy-done((f32[2048,256]{1,0:T(8,128)S(1)}, f32[2048,256]{1,0:T(8,128)}, u32[]{:S(2)}) %copy-start.3) | copy-done | bytes 2097176
  6.4 0.0 copy-start.4
  6.4 0.8 %copy-done.4 = bf16[128,256]{1,0:T(8,128)(2,1)S(1)} copy-done((bf16[128,256]{1,0:T(8,128)(2,1)S(1)}, bf16[128,256]{1,0:T(8,128)(2,1)}, u32[]{:S(2)}) %copy-start.4) | copy-done | bytes 65560
  7.2 0.0 copy-start.7
  7.2 0.0 copy-start.8
  7.2 0.0 copy-start.9
  7.2 69.7 %shard_map.107 = (bf16[128,2048]{1,0:T(8,128)(2,1)S(1)}, bf16[128,256]{1,0:T(8,128)(2,1)S(1)}) custom-call(bf16[128,8192]{1,0:T(8,128)(2,1)S(1)} %bitcast.28, bf16[128,256]{1,0:T(8,128)(2,1)S(1)} %copy-done.4, f32[2048,256]{1,0:T(8,128)S(1)} %copy-done.1, f32[2048,256]{1,0:T(8,128)S(1)} %copy-done.2, f32[2048,256]{1,0:T(8,128)S(1)} %copy-done.3), custom_call_target="tpu_custom_call" | custom-call | tf_op jit(solution)/shard_map/pallas_call | solution.py:350
  77.0 0.0 copy-done.7
  77.0 0.0 copy-done.8
  77.0 0.0 copy-done.9
  77.0 0.8 %copy.76 = bf16[1,128,2048]{2,1,0:T(8,128)(2,1)} copy(bf16[1,128,2048]{2,1,0:T(8,128)(2,1)S(1)} %get-tuple-element.33) | data formatting | bytes 1048576
  (1 shorter events, 0.0 us)
Async XLA Ops:
  0.0 1.6 %copy-start = (bf16[1,128,8192]{2,1,0:T(8,128)(2,1)S(1)}, bf16[1,128,8192]{2,1,0:T(8,128)(2,1)}, u32[]{:S(2)}) copy-start(bf16[1,128,8192]{2,1,0:T(8,128)(2,1)} %param.12) | copy-start | bytes 6291460
  1.6 1.6 %copy-start.1 = (f32[2048,256]{1,0:T(8,128)S(1)}, f32[2048,256]{1,0:T(8,128)}, u32[]{:S(2)}) copy-start(f32[2048,256]{1,0:T(8,128)} %master.1) | copy-start | bytes 6291460
  3.2 1.6 %copy-start.2 = (f32[2048,256]{1,0:T(8,128)S(1)}, f32[2048,256]{1,0:T(8,128)}, u32[]{:S(2)}) copy-start(f32[2048,256]{1,0:T(8,128)} %moment1.1) | copy-start | bytes 6291460
  4.8 1.6 %copy-start.3 = (f32[2048,256]{1,0:T(8,128)S(1)}, f32[2048,256]{1,0:T(8,128)}, u32[]{:S(2)}) copy-start(f32[2048,256]{1,0:T(8,128)} %moment2.1) | copy-start | bytes 6291460
  6.4 0.8 %copy-start.4 = (bf16[128,256]{1,0:T(8,128)(2,1)S(1)}, bf16[128,256]{1,0:T(8,128)(2,1)}, u32[]{:S(2)}) copy-start(bf16[128,256]{1,0:T(8,128)(2,1)} %og.1) | copy-start | bytes 196612
  7.2 69.8 %copy-start.7 = (bf16[8,16,2048]{2,1,0:T(8,128)(2,1)S(1)}, bf16[8,16,2048]{2,1,0:T(8,128)(2,1)}, u32[]{:S(2)}) copy-start(bf16[8,16,2048]{2,1,0:T(8,128)(2,1)} %param.17) | copy-start | bytes 1572868
  7.2 69.8 %copy-start.8 = (bf16[8,16,256]{2,1,0:T(8,128)(2,1)S(1)}, bf16[8,16,256]{2,1,0:T(8,128)(2,1)}, u32[]{:S(2)}) copy-start(bf16[8,16,256]{2,1,0:T(8,128)(2,1)} %param.18) | copy-start | bytes 196612
  7.2 69.8 %copy-start.9 = (s32[16]{0:T(128)S(1)}, s32[16]{0:T(128)}, u32[]{:S(2)}) copy-start(s32[16]{0:T(128)} %param.21) | copy-start | bytes 196

commit v4 on v3

--- a/solution.py
+++ b/solution.py
@@ -76,10 +76,11 @@
 
 
 def fused_kernel(
-    n, m, split, hid, og, master, moment1, moment2, back, vals,
+    n, m, split, hid, og, master, moment1, moment2, queries, keys, k_cache, v_cache, lens, back, att,
     slabs, ogs, master_v, moment1_v, moment2_v, fresh, sums, parts, slots, reduced, val_slots,
     og_send, og_recv, hid_send, hid_recv, loc, x_send, x_recv, c_send, c_recv,
     p_send, p_recv, b_send, b_recv, v_send, v_recv,
+    vals, queries_v, keys_v, k_v, v_v, cache_out, fresh_wts, att_sem,
 ):
     r, i, t = position()
     q = n // m
@@ -99,6 +100,18 @@
     for load in loads:
         load.start()
 
+    att_loads = [
+        pltpu.make_async_copy(src, dst, att_sem.at[k])
+        for k, (src, dst) in enumerate(
+            ((queries, queries_v), (keys, keys_v), (k_cache, k_v), (v_cache, v_v))
+        )
+    ]
+
+    @pl.when(r == 1)
+    def _():
+        for load in att_loads:
+            load.start()
+
     barrier = pltpu.get_barrier_semaphore()
 
     def greet(k):
@@ -148,6 +161,48 @@
 
     og_local = pltpu.make_async_copy(og, ogs.at[i], loc.at[0])
     og_local.start()
+
+    replica_rows, kv_heads, asked = queries.shape[:3]
+    half_rows = replica_rows // 2
+
+    def attend_row(row):
+        for k in range(kv_heads):
+            at = slice(k * HD, (k + 1) * HD)
+            cache_score, fresh_score = [
+                lax.dot_general(
+                    queries_v[row, k], known, (((1,), (1,)), ((), ())), preferred_element_type=jnp.float32
+                )
+                * HD ** (-0.5)
+                for known in (k_v[row, :, at], keys_v[:, at])
+            ]
+            place = lax.broadcasted_iota(jnp.int32, cache_score.shape, 1)
+            cache_score = jnp.where(place < lens[row], cache_score, neg_fill)
+            token = lax.broadcasted_iota(jnp.int32, fresh_score.shape, 1)
+            step = lax.broadcasted_iota(jnp.int32, fresh_score.shape, 0) // (asked // STEPS)
+            seen = (token % replica_rows == row) & (token // replica_rows <= step)
+            fresh_score = jnp.where(seen, fresh_score, neg_fill)
+            top = jnp.maximum(
+                jnp.max(cache_score, axis=-1, keepdims=True), jnp.max(fresh_score, axis=-1, keepdims=True)
+            )
+            cache_exp = jnp.exp(cache_score - top)
+            fresh_exp = jnp.exp(fresh_score - top)
+            total = jnp.sum(cache_exp, axis=-1, keepdims=True) + jnp.sum(fresh_exp, axis=-1, keepdims=True)
+            cache_wts = (cache_exp / total).astype(jnp.bfloat16)
+            fresh_wts[row, k] = (fresh_exp / total).astype(jnp.bfloat16)
+            cache_out[row, k] = jnp.dot(cache_wts, v_v[row, :, at], preferred_element_type=jnp.float32)
+
+    def finish_row(row):
+        for k in range(kv_heads):
+            new = jnp.dot(
+                fresh_wts[row, k], vals[:, k * HD : (k + 1) * HD], preferred_element_type=jnp.float32
+            )
+            att[row, k] = (cache_out[row, k] + new).astype(att.dtype)
+
+    @pl.when(r == 1)
+    def _():
+        for load in att_loads:
+            load.wait()
+        each(half_rows, attend_row)
 
     def to_pair(which, src):
         return remote(
@@ -193,6 +248,10 @@
     og_local.wait()
     for load in loads:
         load.wait()
+
+    @pl.when(r == 1)
+    def _():
+        each(replica_rows - half_rows, lambda k: attend_row(half_rows + k))
 
     chunk = min(512, full)
     block_rows = q * og.shape[0]
@@ -315,6 +374,7 @@
         drain(val_slots.at[pl.ds(0, sources - 1)], v_recv)
         kept.wait()
         total_of(val_slots, sources, vals, 16)
+        each(replica_rows, finish_row)
         drain(val_slots.at[pl.ds(0, n - 1)], v_send)
 
     @pl.when(active)
@@ -337,23 +397,23 @@
     drain(ogs.at[pl.ds(0, n - 1)], og_send)
 
 
-def fused(hid, og, master, moment1, moment2, n, m):
+def fused(hid, og, master, moment1, moment2, queries, keys, k_cache, v_cache, lens, n, m):
     q = n // m
     full, heads = master.shape
     tokens = og.shape[0]
     split = full % 256 == 0
     width = full // 2 if split else full
     dma = pltpu.SemaphoreType.DMA
-    anywhere = pl.BlockSpec(memory_space=pl.ANY)
+    anywhere = pl.BlockSpec(memory_space=pltpu.HBM)
     half = pltpu.VMEM((width, heads), jnp.float32)
     block = pltpu.VMEM((m, q * tokens, full), jnp.bfloat16)
     return pl.pallas_call(
         functools.partial(fused_kernel, n, m, split),
         out_shape=(
             jax.ShapeDtypeStruct((tokens, q * full), jnp.bfloat16),
-            jax.ShapeDtypeStruct((tokens, heads), jnp.bfloat16),
+            jax.ShapeDtypeStruct(queries.shape, jnp.bfloat16),
         ),
-        in_specs=[anywhere] * 5,
+        in_specs=[anywhere] * 9 + [pl.BlockSpec(memory_space=pltpu.SMEM)],
         out_specs=(anywhere, pl.BlockSpec(memory_space=pltpu.VMEM)),
         scratch_shapes=[
             pltpu.VMEM((2, m, n, tokens // m, width), jnp.bfloat16),
@@ -370,11 +430,19 @@
             dma, dma, dma((2,)), dma((2,)), dma((5,)),
             dma((2, m // 2)), dma((2, m // 2)), dma((2, m // 2)), dma((2, m // 2)),
             dma, dma, dma, dma, dma, dma,
+            pltpu.VMEM((tokens, heads), jnp.bfloat16),
+            pltpu.VMEM(queries.shape, queries.dtype),
+            pltpu.VMEM(keys.shape, keys.dtype),
+            pltpu.VMEM(k_cache.shape, k_cache.dtype),
+            pltpu.VMEM(v_cache.shape, v_cache.dtype),
+            pltpu.VMEM(queries.shape, jnp.float32),
+            pltpu.VMEM(queries.shape[:3] + (tokens,), jnp.bfloat16),
+            dma((4,)),
         ],
         compiler_params=pltpu.CompilerParams(
-            collective_id=0, has_side_effects=True, vmem_limit_bytes=40 * 2**20
+            collective_id=0, has_side_effects=True, vmem_limit_bytes=60 * 2**20
         ),
-    )(hid, og, master, moment1, moment2)
+    )(hid, og, master, moment1, moment2, queries, keys, k_cache, v_cache, lens)
 
 
 def local(
@@ -382,51 +450,27 @@
 ):
     is_learner = lax.axis_index("role") == 0
     n, m = lax.axis_size("dp"), lax.axis_size("tp")
-    learner_rows, values = fused(hidden[0], out_grad, master, moment1, moment2, n, m)
-    result = lax.cond(
-        is_learner,
-        lambda: learner_rows,
-        lambda: attend(values, queries, new_keys, k_cache, v_cache, cache_len),
+    replica_rows = cache_len.shape[0]
+    heads_here = out_grad.shape[1] // HD
+    share = QH // KVH
+    asked = queries.reshape(STEPS, replica_rows, heads_here, share, HD).transpose(1, 2, 0, 3, 4)
+    learner_rows, attended = fused(
+        hidden[0],
+        out_grad,
+        master,
+        moment1,
+        moment2,
+        asked.reshape(replica_rows, heads_here, STEPS * share, HD),
+        new_keys.reshape(STEPS * replica_rows, heads_here * HD),
+        k_cache,
+        v_cache,
+        cache_len,
+        n,
+        m,
     )
+    decoded = attended.reshape(replica_rows, heads_here, STEPS, share, HD).transpose(2, 0, 1, 3, 4)
+    result = jnp.where(is_learner, learner_rows, decoded.reshape(learner_rows.shape))
     return result[None]
-
-
-def attend(values, queries, new_keys, k_cache, v_cache, cache_len):
-    heads_here = values.shape[1] // HD
-    share = QH // KVH
-    replica_rows = cache_len.shape[0]
-    cache_size = k_cache.shape[1]
-    values = values.reshape(STEPS, replica_rows, heads_here, HD)
-    query_all = queries.reshape(STEPS, replica_rows, heads_here, share, HD)
-    newkey_all = new_keys.reshape(STEPS, replica_rows, heads_here, HD)
-    cache_keys = k_cache.reshape(replica_rows, cache_size, heads_here, HD)
-    cache_vals = v_cache.reshape(replica_rows, cache_size, heads_here, HD)
-    scale = HD ** (-0.5)
-    cache_score = (
-        jnp.einsum("srkgd,rpkd->srkgp", query_all, cache_keys, preferred_element_type=jnp.float32)
-        * scale
-    )
-    valid = jnp.arange(cache_size)[None, :] < cache_len[:, None]
-    cache_score = jnp.where(valid[None, :, None, None, :], cache_score, neg_fill)
-    fresh_score = (
-        jnp.einsum("srkgd,trkd->srkgt", query_all, newkey_all, preferred_element_type=jnp.float32)
-        * scale
-    )
-    causal = jnp.arange(STEPS)[:, None] >= jnp.arange(STEPS)[None, :]
-    fresh_score = jnp.where(causal[:, None, None, None, :], fresh_score, neg_fill)
-    top = jnp.maximum(jnp.max(cache_score, axis=-1), jnp.max(fresh_score, axis=-1))
-    cache_exp = jnp.exp(cache_score - top[..., None])
-    fresh_exp = jnp.exp(fresh_score - top[..., None])
-    total = jnp.sum(cache_exp, axis=-1) + jnp.sum(fresh_exp, axis=-1)
-    cache_wts = (cache_exp / total[..., None]).astype(jnp.bfloat16)
-    fresh_wts = (fresh_exp / total[..., None]).astype(jnp.bfloat16)
-    output = jnp.einsum(
-        "srkgp,rpkd->srkgd", cache_wts, cache_vals, preferred_element_type=jnp.float32
-    )
-    output = output + jnp.einsum(
-        "srkgt,trkd->srkgd", fresh_wts, values, preferred_element_type=jnp.float32
-    )
-    return output.astype(jnp.bfloat16).reshape(STEPS * replica_rows, heads_here * share * HD)
 
 
 def solution(mesh):

time: 78.2 us -> 75.9 us (0.971)
  local copies, waits for them, and re-layouts: 8.01 us -> 3.51 us
  Pallas kernels: 69.7 us -> 71.3 us
  other arithmetic: 0 us -> 0.85 us
    unnamed x17 -> x3, local copies, waits for them, and re-layouts: 8.01 us -> 1.15 us
    pallas_call x1, Pallas kernels: 69.7 us -> 71.3 us  [fused(): pl.pallas_call(functools.partial(fused_kernel, n, m, split), out_shape=(j...]
    transpose x0 -> x1, local copies, waits for them, and re-layouts: none -> 1.19 us  [local(): attended.reshape(replica_rows, heads_here, STEPS, share, HD)]
    reshape x0 -> x2, local copies, waits for them, and re-layouts: none -> 1.17 us  [the longest x1 0.94 us: local(): queries.reshape(STEPS, replica_rows, heads_here, share, HD)]
    broadcast_in_dim x0 -> x1, other arithmetic: none -> 0.85 us  [local(): return result[None]]
where the time goes in v4:
time: 75.9 us; the launch traced here: 75.7 us
  Pallas kernels  71.3 us (94%)
  local copies, waits for them, and re-layouts  3.51 us (5%)
  other arithmetic  0.85 us (1%)
    pallas_call x1, Pallas kernels, fused(): pl.pallas_call(functools.partial(fused_kernel, n, m, split), out_shape=(j...  71.3 us

profile of v4, /device:TPU:25, one launch (start us, length us, event | category | flops | bytes accessed | tf_op | source)
XLA Modules:
  0.0 75.7 jit_solution(565564758447998389)
XLA Ops:
  0.0 1.1 %copy.13 = bf16[16,8,16,128]{3,2,1,0:T(8,128)(2,1)S(1)} copy(bf16[16,8,16,128]{3,1,2,0:T(8,128)(2,1)} %bitcast.21) | data formatting | bytes 1048576
  1.2 0.9 %copy.15 = bf16[8,16,2,8,128]{4,3,0,2,1:T(8,128)(2,1)} copy(bf16[8,16,2,8,128]{4,3,2,1,0:T(8,128)(2,1)S(1)} %bitcast.20) | data formatting | bytes 1048576 | tf_op jit(solution)/shard_map/reshape | solution.py:456
  2.1 71.3 %shard_map.100 = (bf16[128,2048]{1,0:T(8,128)(2,1)}, bf16[16,2,64,128]{3,2,1,0:T(8,128)(2,1)}) custom-call(bf16[128,8192]{1,0:T(8,128)(2,1)} %bitcast.18, bf16[128,256]{1,0:T(8,128)(2,1)} %og.1, f32[2048,256]{1,0:T(8,128)} %master.1, f32[2048,256]{1,0:T(8,128)} %moment1.1, f32[2048,256]{1,0:T(8,128)} %moment2.1, bf16[16,2,64,128]{3,2,1,0:T(8,128)(2,1)} %bitcast.19, ...), custom_call_target="tpu_custom_call" | custom-call | tf_op jit(solution)/shard_map/pallas_call | solution.py:410
  73.4 0.0 copy-start
  73.4 1.2 %copy.12 = bf16[8,16,2,8,128]{4,3,2,1,0:T(8,128)(2,1)S(1)} copy(bf16[8,16,2,8,128]{4,3,0,2,1:T(8,128)(2,1)} %bitcast.22) | data formatting | bytes 1048576 | tf_op jit(solution)/shard_map/transpose | solution.py:471
  74.6 0.2 reshape.19
  74.8 0.0 copy-done
  74.8 0.9 %select_bitcast_fusion = bf16[1,128,2048]{2,1,0:T(8,128)(2,1)} fusion(bf16[128,2048]{1,0:T(8,128)(2,1)S(1)} %copy-done, bf16[128,2048]{1,0:T(8,128)(2,1)S(1)} %reshape.19, pred[]{:T(512)S(6)} %eq.3), kind=kLoop, calls=%fused_computation.1 | loop fusion | flops 262144 | bytes 1572865 | tf_op jit(solution)/shard_map/broadcast_in_dim | solution.py:473
Async XLA Ops:
  73.4 1.4 %copy-start = (bf16[128,2048]{1,0:T(8,128)(2,1)S(1)}, bf16[128,2048]{1,0:T(8,128)(2,1)}, u32[]{:S(2)}) copy-start(bf16[128,2048]{1,0:T(8,128)(2,1)} %get-tuple-element.7) | copy-start | bytes 1572868

commit v5 on v4

--- a/solution.py
+++ b/solution.py
@@ -127,6 +127,8 @@
         def _():
             signal(barrier, 0, t * q + k, home)
 
+        signal(barrier, 1, t * q + k, home)
+
     each(2 * n, greet)
     each(m - 1, greet_tp)
 
@@ -137,7 +139,7 @@
 
     @pl.when(r == 1)
     def _():
-        pl.semaphore_wait(barrier, 2 * n - 1 + m - 1)
+        pl.semaphore_wait(barrier, 2 * n - 1 + m - 1 + q)
 
     def piece(role, j):
         start = j * full + (role * width if split else 0)
@@ -249,15 +251,13 @@
     for load in loads:
         load.wait()
 
-    @pl.when(r == 1)
-    def _():
-        each(replica_rows - half_rows, lambda k: attend_row(half_rows + k))
-
     chunk = min(512, full)
-    block_rows = q * og.shape[0]
+    part_rows = og.shape[0] // 2
+    block_rows = q * part_rows
+    own_half = pl.ds(pl.multiple_of(r * part_rows, part_rows), part_rows)
 
     def fill_part(g):
-        tokens = ogs[pl.ds(g * q, q)].reshape(block_rows, heads)
+        tokens = ogs[pl.ds(g * q, q), own_half, :].reshape(block_rows, heads)
 
         def columns(k):
             at = pl.ds(pl.multiple_of(k * chunk, chunk), chunk)
@@ -272,16 +272,18 @@
 
     mine = pltpu.make_async_copy(parts.at[t], slots.at[t], loc.at[0])
 
-    @pl.when(r == 0)
-    def _():
-        def send_part(k):
-            g = (t + 1 + k) % m
-            fill_part(g)
-            remote(parts.at[g], slots.at[t], p_send, p_recv, 0, i, g).start()
-
-        each(m - 1, send_part)
-        fill_part(t)
-        mine.start()
+    def send_part(k):
+        g = (t + 1 + k) % m
+        fill_part(g)
+        remote(parts.at[g], slots.at[t], p_send, p_recv, r, i, g).start()
+
+    each(m - 1, send_part)
+    fill_part(t)
+    mine.start()
+
+    @pl.when(r == 1)
+    def _():
+        each(replica_rows - half_rows, lambda k: attend_row(half_rows + k))
 
     def send_sum(j):
         slot = r * n + i if split else i
@@ -329,41 +331,40 @@
         def _():
             send_sum(i)
 
+    drain(slots.at[pl.ds(0, m - 1)], p_recv)
+    mine.wait()
+    total_of(slots, m, reduced, 16)
+
+    def place(j):
+        return back.at[own_half, pl.ds(pl.multiple_of((j % q) * full, full), full)]
+
+    def block(k):
+        return reduced.at[pl.ds(pl.multiple_of(k * part_rows, part_rows), part_rows)]
+
+    def send_block(k):
+        @pl.when((r == 1) | (t * q + k != i))
+        def _():
+            remote(block(k), place(i), b_send, b_recv, 0, t * q + k, home).start()
+
+    each(q, send_block)
+
+    @pl.when((r == 0) & (home == t))
+    def _():
+        keep = pltpu.make_async_copy(block(i % q), place(i), loc.at[0])
+        keep.start()
+        keep.wait()
+        drain(reduced, b_recv)
+        if q > 1:
+            drain(reduced.at[pl.ds(0, (q - 1) * part_rows)], b_recv)
+            drain(reduced.at[pl.ds(0, (q - 1) * part_rows)], b_send)
+
+    @pl.when((r == 0) & (home != t))
+    def _():
+        drain(back, b_recv)
+        drain(reduced, b_send)
+
     @pl.when(r == 0)
     def _():
-        drain(slots.at[pl.ds(0, m - 1)], p_recv)
-        mine.wait()
-        total_of(slots, m, reduced, 16)
-        size = back.shape[0]
-
-        def place(j):
-            return back.at[:, pl.ds(pl.multiple_of((j % q) * full, full), full)]
-
-        def block(k):
-            return reduced.at[pl.ds(pl.multiple_of(k * size, size), size)]
-
-        def send_block(k):
-            @pl.when(t * q + k != i)
-            def _():
-                remote(block(k), place(i), b_send, b_recv, 0, t * q + k, home).start()
-
-        each(q, send_block)
-
-        @pl.when(home == t)
-        def _():
-            keep = pltpu.make_async_copy(block(i % q), place(i), loc.at[0])
-            keep.start()
-            keep.wait()
-            if q > 1:
-                drain(reduced.at[pl.ds(0, (q - 1) * size)], b_recv)
-                drain(reduced.at[pl.ds(0, (q - 1) * size)], b_send)
-
-        @pl.when(home != t)
-        def _():
-            drain(reduced, b_recv)
-            drain(reduced, b_send)
-
-        drain(slots.at[pl.ds(0, m - 1)], p_send)
         if split:
             drain(val_slots.at[pl.ds(0, n)], v_send)
 
@@ -376,6 +377,9 @@
         total_of(val_slots, sources, vals, 16)
         each(replica_rows, finish_row)
         drain(val_slots.at[pl.ds(0, n - 1)], v_send)
+        drain(reduced, b_send)
+
+    drain(slots.at[pl.ds(0, m - 1)], p_send)
 
     @pl.when(active)
     def _():
@@ -406,7 +410,7 @@
     dma = pltpu.SemaphoreType.DMA
     anywhere = pl.BlockSpec(memory_space=pltpu.HBM)
     half = pltpu.VMEM((width, heads), jnp.float32)
-    block = pltpu.VMEM((m, q * tokens, full), jnp.bfloat16)
+    block = pltpu.VMEM((m, q * (tokens // 2), full), jnp.bfloat16)
     return pl.pallas_call(
         functools.partial(fused_kernel, n, m, split),
         out_shape=(
@@ -425,7 +429,7 @@
             pltpu.VMEM((n, tokens, heads), jnp.bfloat16),
             block,
             block,
-            pltpu.VMEM((q * tokens, full), jnp.bfloat16),
+            pltpu.VMEM((q * (tokens // 2), full), jnp.bfloat16),
             pltpu.VMEM((n * (2 if split else 1), tokens, heads), jnp.bfloat16),
             dma, dma, dma((2,)), dma((2,)), dma((5,)),
             dma((2, m // 2)), dma((2, m // 2)), dma((2, m // 2)), dma((2, m // 2)),

time: 75.9 us -> 64.3 us (0.85)
  the two profiles are of different devices: /device:TPU:25 before, /device:TPU:2 now
where the time goes in v5:
time: 64.3 us; the launch traced here: 64.1 us
  Pallas kernels  59.7 us (93%)
  local copies, waits for them, and re-layouts  3.51 us (5%)
  other arithmetic  0.85 us (1%)
    pallas_call x1, Pallas kernels, fused(): pl.pallas_call(functools.partial(fused_kernel, n, m, split), out_shape=(j...  59.7 us

profile of v5, /device:TPU:2, one launch (start us, length us, event | category | flops | bytes accessed | tf_op | source)
XLA Modules:
  0.0 64.1 jit_solution(14907700287582696912)
XLA Ops:
  0.0 1.1 %copy.13 = bf16[16,8,16,128]{3,2,1,0:T(8,128)(2,1)S(1)} copy(bf16[16,8,16,128]{3,1,2,0:T(8,128)(2,1)} %bitcast.21) | data formatting | bytes 1048576
  1.2 0.9 %copy.15 = bf16[8,16,2,8,128]{4,3,0,2,1:T(8,128)(2,1)} copy(bf16[8,16,2,8,128]{4,3,2,1,0:T(8,128)(2,1)S(1)} %bitcast.20) | data formatting | bytes 1048576 | tf_op jit(solution)/shard_map/reshape | solution.py:460
  2.1 59.7 %shard_map.100 = (bf16[128,2048]{1,0:T(8,128)(2,1)}, bf16[16,2,64,128]{3,2,1,0:T(8,128)(2,1)}) custom-call(bf16[128,8192]{1,0:T(8,128)(2,1)} %bitcast.18, bf16[128,256]{1,0:T(8,128)(2,1)} %og.1, f32[2048,256]{1,0:T(8,128)} %master.1, f32[2048,256]{1,0:T(8,128)} %moment1.1, f32[2048,256]{1,0:T(8,128)} %moment2.1, bf16[16,2,64,128]{3,2,1,0:T(8,128)(2,1)} %bitcast.19, ...), custom_call_target="tpu_custom_call" | custom-call | tf_op jit(solution)/shard_map/pallas_call | solution.py:414
  61.8 0.0 copy-start
  61.8 1.2 %copy.12 = bf16[8,16,2,8,128]{4,3,2,1,0:T(8,128)(2,1)S(1)} copy(bf16[8,16,2,8,128]{4,3,0,2,1:T(8,128)(2,1)} %bitcast.22) | data formatting | bytes 1048576 | tf_op jit(solution)/shard_map/transpose | solution.py:475
  63.0 0.2 reshape.19
  63.2 0.0 copy-done
  63.2 0.9 %select_bitcast_fusion = bf16[1,128,2048]{2,1,0:T(8,128)(2,1)} fusion(bf16[128,2048]{1,0:T(8,128)(2,1)S(1)} %copy-done, bf16[128,2048]{1,0:T(8,128)(2,1)S(1)} %reshape.19, pred[]{:T(512)S(6)} %eq.3), kind=kLoop, calls=%fused_computation.1 | loop fusion | flops 262144 | bytes 1572865 | tf_op jit(solution)/shard_map/broadcast_in_dim | solution.py:477
Async XLA Ops:
  61.8 1.4 %copy-start = (bf16[128,2048]{1,0:T(8,128)(2,1)S(1)}, bf16[128,2048]{1,0:T(8,128)(2,1)}, u32[]{:S(2)}) copy-start(bf16[128,2048]{1,0:T(8,128)(2,1)} %get-tuple-element.7) | copy-start | bytes 1572868

commit v6 on v5

--- a/solution.py
+++ b/solution.py
@@ -315,6 +315,26 @@
             fresh[at, :] = adam_fresh(master_v[held, :], moment1_v[at, :], moment2_v[at, :], gradient)
 
         each(width // tile, update)
+
+    drain(slots.at[pl.ds(0, m - 1)], p_recv)
+    mine.wait()
+    total_of(slots, m, reduced, 16)
+
+    def place(j):
+        return back.at[own_half, pl.ds(pl.multiple_of((j % q) * full, full), full)]
+
+    def block(k):
+        return reduced.at[pl.ds(pl.multiple_of(k * part_rows, part_rows), part_rows)]
+
+    def send_block(k):
+        @pl.when((r == 1) | (t * q + k != i))
+        def _():
+            remote(block(k), place(i), b_send, b_recv, 0, t * q + k, home).start()
+
+    each(q, send_block)
+
+    @pl.when(active)
+    def _():
         for src in range(pairs):
             from_pair(1, src)
         for g in range(m):
@@ -330,23 +350,6 @@
         @pl.when(r == 0)
         def _():
             send_sum(i)
-
-    drain(slots.at[pl.ds(0, m - 1)], p_recv)
-    mine.wait()
-    total_of(slots, m, reduced, 16)
-
-    def place(j):
-        return back.at[own_half, pl.ds(pl.multiple_of((j % q) * full, full), full)]
-
-    def block(k):
-        return reduced.at[pl.ds(pl.multiple_of(k * part_rows, part_rows), part_rows)]
-
-    def send_block(k):
-        @pl.when((r == 1) | (t * q + k != i))
-        def _():
-            remote(block(k), place(i), b_send, b_recv, 0, t * q + k, home).start()
-
-    each(q, send_block)
 
     @pl.when((r == 0) & (home == t))
     def _():

time: 64.3 us -> 69.9 us (1.087)
  the two profiles are of different devices: /device:TPU:2 before, /device:TPU:5 now
where the time goes in v6:
time: 69.9 us; the launch traced here: 69.7 us
  Pallas kernels  65.3 us (93%)
  local copies, waits for them, and re-layouts  3.51 us (5%)
  other arithmetic  0.85 us (1%)
    pallas_call x1, Pallas kernels, fused(): pl.pallas_call(functools.partial(fused_kernel, n, m, split), out_shape=(j...  65.3 us

profile of v6, /device:TPU:5, one launch (start us, length us, event | category | flops | bytes accessed | tf_op | source)
XLA Modules:
  0.0 69.7 jit_solution(5357614476858603706)
XLA Ops:
  0.0 1.1 %copy.13 = bf16[16,8,16,128]{3,2,1,0:T(8,128)(2,1)S(1)} copy(bf16[16,8,16,128]{3,1,2,0:T(8,128)(2,1)} %bitcast.21) | data formatting | bytes 1048576
  1.2 0.9 %copy.15 = bf16[8,16,2,8,128]{4,3,0,2,1:T(8,128)(2,1)} copy(bf16[8,16,2,8,128]{4,3,2,1,0:T(8,128)(2,1)S(1)} %bitcast.20) | data formatting | bytes 1048576 | tf_op jit(solution)/shard_map/reshape | solution.py:463
  2.1 65.3 %shard_map.100 = (bf16[128,2048]{1,0:T(8,128)(2,1)}, bf16[16,2,64,128]{3,2,1,0:T(8,128)(2,1)}) custom-call(bf16[128,8192]{1,0:T(8,128)(2,1)} %bitcast.18, bf16[128,256]{1,0:T(8,128)(2,1)} %og.1, f32[2048,256]{1,0:T(8,128)} %master.1, f32[2048,256]{1,0:T(8,128)} %moment1.1, f32[2048,256]{1,0:T(8,128)} %moment2.1, bf16[16,2,64,128]{3,2,1,0:T(8,128)(2,1)} %bitcast.19, ...), custom_call_target="tpu_custom_call" | custom-call | tf_op jit(solution)/shard_map/pallas_call | solution.py:417
  67.4 0.0 copy-start
  67.4 1.2 %copy.12 = bf16[8,16,2,8,128]{4,3,2,1,0:T(8,128)(2,1)S(1)} copy(bf16[8,16,2,8,128]{4,3,0,2,1:T(8,128)(2,1)} %bitcast.22) | data formatting | bytes 1048576 | tf_op jit(solution)/shard_map/transpose | solution.py:478
  68.6 0.2 reshape.19
  68.9 0.0 copy-done
  68.9 0.9 %select_bitcast_fusion = bf16[1,128,2048]{2,1,0:T(8,128)(2,1)} fusion(bf16[128,2048]{1,0:T(8,128)(2,1)S(1)} %copy-done, bf16[128,2048]{1,0:T(8,128)(2,1)S(1)} %reshape.19, pred[]{:T(512)S(6)} %eq.3), kind=kLoop, calls=%fused_computation.1 | loop fusion | flops 262144 | bytes 1572865 | tf_op jit(solution)/shard_map/broadcast_in_dim | solution.py:480
Async XLA Ops:
  67.4 1.4 %copy-start = (bf16[128,2048]{1,0:T(8,128)(2,1)S(1)}, bf16[128,2048]{1,0:T(8,128)(2,1)}, u32[]{:S(2)}) copy-start(bf16[128,2048]{1,0:T(8,128)(2,1)} %get-tuple-element.7) | copy-start | bytes 1572868

commit v7 on v5

--- a/solution.py
+++ b/solution.py
@@ -200,6 +200,41 @@
             )
             att[row, k] = (cache_out[row, k] + new).astype(att.dtype)
 
+    drain(ogs.at[pl.ds(0, n - 1)], og_recv)
+    og_local.wait()
+    for load in loads:
+        load.wait()
+
+    chunk = min(512, full)
+    part_rows = og.shape[0] // 2
+    block_rows = q * part_rows
+    own_half = pl.ds(pl.multiple_of(r * part_rows, part_rows), part_rows)
+
+    def fill_part(g):
+        tokens = ogs[pl.ds(g * q, q), own_half, :].reshape(block_rows, heads)
+
+        def columns(k):
+            at = pl.ds(pl.multiple_of(k * chunk, chunk), chunk)
+            parts[g, :, at] = lax.dot_general(
+                tokens,
+                master_v[at, :].astype(jnp.bfloat16),
+                (((1,), (1,)), ((), ())),
+                preferred_element_type=jnp.float32,
+            ).astype(jnp.bfloat16)
+
+        each(full // chunk, columns)
+
+    mine = pltpu.make_async_copy(parts.at[t], slots.at[t], loc.at[0])
+
+    def send_part(k):
+        g = (t + 1 + k) % m
+        fill_part(g)
+        remote(parts.at[g], slots.at[t], p_send, p_recv, r, i, g).start()
+
+    each(m - 1, send_part)
+    fill_part(t)
+    mine.start()
+
     @pl.when(r == 1)
     def _():
         for load in att_loads:
@@ -245,41 +280,6 @@
             for step in range(1, pairs):
                 over(which, step).start()
             to_pair(which, px).start()
-
-    drain(ogs.at[pl.ds(0, n - 1)], og_recv)
-    og_local.wait()
-    for load in loads:
-        load.wait()
-
-    chunk = min(512, full)
-    part_rows = og.shape[0] // 2
-    block_rows = q * part_rows
-    own_half = pl.ds(pl.multiple_of(r * part_rows, part_rows), part_rows)
-
-    def fill_part(g):
-        tokens = ogs[pl.ds(g * q, q), own_half, :].reshape(block_rows, heads)
-
-        def columns(k):
-            at = pl.ds(pl.multiple_of(k * chunk, chunk), chunk)
-            parts[g, :, at] = lax.dot_general(
-                tokens,
-                master_v[at, :].astype(jnp.bfloat16),
-                (((1,), (1,)), ((), ())),
-                preferred_element_type=jnp.float32,
-            ).astype(jnp.bfloat16)
-
-        each(full // chunk, columns)
-
-    mine = pltpu.make_async_copy(parts.at[t], slots.at[t], loc.at[0])
-
-    def send_part(k):
-        g = (t + 1 + k) % m
-        fill_part(g)
-        remote(parts.at[g], slots.at[t], p_send, p_recv, r, i, g).start()
-
-    each(m - 1, send_part)
-    fill_part(t)
-    mine.start()
 
     @pl.when(r == 1)
     def _():

time: 64.3 us -> 63.1 us (0.981)
  Pallas kernels: 59.7 us -> 58.5 us
    pallas_call x1, Pallas kernels: 59.7 us -> 58.5 us  [fused(): pl.pallas_call(functools.partial(fused_kernel, n, m, split), out_shape=(j...]
where the time goes in v7:
time: 63.1 us; the launch traced here: 62.9 us
  Pallas kernels  58.5 us (93%)
  local copies, waits for them, and re-layouts  3.51 us (6%)
  other arithmetic  0.85 us (1%)
    pallas_call x1, Pallas kernels, fused(): pl.pallas_call(functools.partial(fused_kernel, n, m, split), out_shape=(j...  58.5 us

profile of v7, /device:TPU:2, one launch (start us, length us, event | category | flops | bytes accessed | tf_op | source)
XLA Modules:
  0.0 62.9 jit_solution(2246277847575966092)
XLA Ops:
  0.0 1.1 %copy.13 = bf16[16,8,16,128]{3,2,1,0:T(8,128)(2,1)S(1)} copy(bf16[16,8,16,128]{3,1,2,0:T(8,128)(2,1)} %bitcast.21) | data formatting | bytes 1048576
  1.2 0.9 %copy.15 = bf16[8,16,2,8,128]{4,3,0,2,1:T(8,128)(2,1)} copy(bf16[8,16,2,8,128]{4,3,2,1,0:T(8,128)(2,1)S(1)} %bitcast.20) | data formatting | bytes 1048576 | tf_op jit(solution)/shard_map/reshape | solution.py:460
  2.1 58.5 %shard_map.100 = (bf16[128,2048]{1,0:T(8,128)(2,1)}, bf16[16,2,64,128]{3,2,1,0:T(8,128)(2,1)}) custom-call(bf16[128,8192]{1,0:T(8,128)(2,1)} %bitcast.18, bf16[128,256]{1,0:T(8,128)(2,1)} %og.1, f32[2048,256]{1,0:T(8,128)} %master.1, f32[2048,256]{1,0:T(8,128)} %moment1.1, f32[2048,256]{1,0:T(8,128)} %moment2.1, bf16[16,2,64,128]{3,2,1,0:T(8,128)(2,1)} %bitcast.19, ...), custom_call_target="tpu_custom_call" | custom-call | tf_op jit(solution)/shard_map/pallas_call | solution.py:414
  60.6 0.0 copy-start
  60.7 1.2 %copy.12 = bf16[8,16,2,8,128]{4,3,2,1,0:T(8,128)(2,1)S(1)} copy(bf16[8,16,2,8,128]{4,3,0,2,1:T(8,128)(2,1)} %bitcast.22) | data formatting | bytes 1048576 | tf_op jit(solution)/shard_map/transpose | solution.py:475
  61.8 0.2 reshape.19
  62.1 0.0 copy-done
  62.1 0.9 %select_bitcast_fusion = bf16[1,128,2048]{2,1,0:T(8,128)(2,1)} fusion(bf16[128,2048]{1,0:T(8,128)(2,1)S(1)} %copy-done, bf16[128,2048]{1,0:T(8,128)(2,1)S(1)} %reshape.19, pred[]{:T(512)S(6)} %eq.3), kind=kLoop, calls=%fused_computation.1 | loop fusion | flops 262144 | bytes 1572865 | tf_op jit(solution)/shard_map/broadcast_in_dim | solution.py:477
Async XLA Ops:
  60.6 1.4 %copy-start = (bf16[128,2048]{1,0:T(8,128)(2,1)S(1)}, bf16[128,2048]{1,0:T(8,128)(2,1)}, u32[]{:S(2)}) copy-start(bf16[128,2048]{1,0:T(8,128)(2,1)} %get-tuple-element.7) | copy-start | bytes 1572868

commit v8 on v7

--- a/solution.py
+++ b/solution.py
@@ -80,7 +80,7 @@
     slabs, ogs, master_v, moment1_v, moment2_v, fresh, sums, parts, slots, reduced, val_slots,
     og_send, og_recv, hid_send, hid_recv, loc, x_send, x_recv, c_send, c_recv,
     p_send, p_recv, b_send, b_recv, v_send, v_recv,
-    vals, queries_v, keys_v, k_v, v_v, cache_out, fresh_wts, att_sem,
+    vals, queries_v, asked_v, keys_v, k_v, v_v, cache_out, fresh_wts, att_sem,
 ):
     r, i, t = position()
     q = n // m
@@ -164,7 +164,8 @@
     og_local = pltpu.make_async_copy(og, ogs.at[i], loc.at[0])
     og_local.start()
 
-    replica_rows, kv_heads, asked = queries.shape[:3]
+    replica_rows, kv_heads, asked = asked_v.shape[:3]
+    share = asked // STEPS
     half_rows = replica_rows // 2
 
     def attend_row(row):
@@ -172,7 +173,7 @@
             at = slice(k * HD, (k + 1) * HD)
             cache_score, fresh_score = [
                 lax.dot_general(
-                    queries_v[row, k], known, (((1,), (1,)), ((), ())), preferred_element_type=jnp.float32
+                    asked_v[row, k].astype(jnp.bfloat16), known, (((1,), (1,)), ((), ())), preferred_element_type=jnp.float32
                 )
                 * HD ** (-0.5)
                 for known in (k_v[row, :, at], keys_v[:, at])
@@ -180,7 +181,7 @@
             place = lax.broadcasted_iota(jnp.int32, cache_score.shape, 1)
             cache_score = jnp.where(place < lens[row], cache_score, neg_fill)
             token = lax.broadcasted_iota(jnp.int32, fresh_score.shape, 1)
-            step = lax.broadcasted_iota(jnp.int32, fresh_score.shape, 0) // (asked // STEPS)
+            step = lax.broadcasted_iota(jnp.int32, fresh_score.shape, 0) // share
             seen = (token % replica_rows == row) & (token // replica_rows <= step)
             fresh_score = jnp.where(seen, fresh_score, neg_fill)
             top = jnp.maximum(
@@ -239,6 +240,13 @@
     def _():
         for load in att_loads:
             load.wait()
+
+        for s in range(STEPS):
+            for k in range(kv_heads):
+                for h in range(share):
+                    at = (k * share + h) * HD
+                    asked_v[:, k, s * share + h, :] = queries_v[s, :, at : at + HD].astype(jnp.float32)
+
         each(half_rows, attend_row)
 
     def to_pair(which, src):
@@ -409,13 +417,14 @@
     width = full // 2 if split else full
     dma = pltpu.SemaphoreType.DMA
     anywhere = pl.BlockSpec(memory_space=pltpu.HBM)
+    asked = (lens.shape[0], heads // HD, STEPS * (QH // KVH), HD)
     half = pltpu.VMEM((width, heads), jnp.float32)
     block = pltpu.VMEM((m, q * (tokens // 2), full), jnp.bfloat16)
     return pl.pallas_call(
         functools.partial(fused_kernel, n, m, split),
         out_shape=(
             jax.ShapeDtypeStruct((tokens, q * full), jnp.bfloat16),
-            jax.ShapeDtypeStruct(queries.shape, jnp.bfloat16),
+            jax.ShapeDtypeStruct(asked, jnp.bfloat16),
         ),
         in_specs=[anywhere] * 9 + [pl.BlockSpec(memory_space=pltpu.SMEM)],
         out_specs=(anywhere, pl.BlockSpec(memory_space=pltpu.VMEM)),
@@ -436,11 +445,12 @@
             dma, dma, dma, dma, dma, dma,
             pltpu.VMEM((tokens, heads), jnp.bfloat16),
             pltpu.VMEM(queries.shape, queries.dtype),
+            pltpu.VMEM(asked, jnp.float32),
             pltpu.VMEM(keys.shape, keys.dtype),
             pltpu.VMEM(k_cache.shape, k_cache.dtype),
             pltpu.VMEM(v_cache.shape, v_cache.dtype),
-            pltpu.VMEM(queries.shape, jnp.float32),
-            pltpu.VMEM(queries.shape[:3] + (tokens,), jnp.bfloat16),
+            pltpu.VMEM(asked, jnp.float32),
+            pltpu.VMEM(asked[:3] + (tokens,), jnp.bfloat16),
             dma((4,)),
         ],
         compiler_params=pltpu.CompilerParams(
@@ -457,14 +467,13 @@
     replica_rows = cache_len.shape[0]
     heads_here = out_grad.shape[1] // HD
     share = QH // KVH
-    asked = queries.reshape(STEPS, replica_rows, heads_here, share, HD).transpose(1, 2, 0, 3, 4)
     learner_rows, attended = fused(
         hidden[0],
         out_grad,
         master,
         moment1,
         moment2,
-        asked.reshape(replica_rows, heads_here, STEPS * share, HD),
+        queries,
         new_keys.reshape(STEPS * replica_rows, heads_here * HD),
         k_cache,
         v_cache,

time: 63.1 us -> 61 us (0.967)
  local copies, waits for them, and re-layouts: 3.51 us -> 1.42 us
    unnamed x3 -> x2, local copies, waits for them, and re-layouts: 1.15 us -> 0.01 us
    reshape x1 -> x0, local copies, waits for them, and re-layouts: 0.94 us -> none  [local(): queries.reshape(STEPS, replica_rows, heads_here, share, HD)]
where the time goes in v8:
time: 61 us; the launch traced here: 60.9 us
  Pallas kernels  58.6 us (96%)
  local copies, waits for them, and re-layouts  1.42 us (2%)
  other arithmetic  0.85 us (1%)
    pallas_call x1, Pallas kernels, fused(): pl.pallas_call(functools.partial(fused_kernel, n, m, split), out_shape=(j...  58.6 us

profile of v8, /device:TPU:2, one launch (start us, length us, event | category | flops | bytes accessed | tf_op | source)
XLA Modules:
  0.0 60.9 jit_solution(12770976727817400989)
XLA Ops:
  0.0 58.6 %shard_map.100 = (bf16[128,2048]{1,0:T(8,128)(2,1)}, bf16[16,2,64,128]{3,2,1,0:T(8,128)(2,1)}) custom-call(bf16[128,8192]{1,0:T(8,128)(2,1)} %bitcast.9, bf16[128,256]{1,0:T(8,128)(2,1)} %og.1, f32[2048,256]{1,0:T(8,128)} %master.1, f32[2048,256]{1,0:T(8,128)} %moment1.1, f32[2048,256]{1,0:T(8,128)} %moment2.1, bf16[8,16,2048]{2,1,0:T(8,128)(2,1)} %queries.1, ...), custom_call_target="tpu_custom_call" | custom-call | tf_op jit(solution)/shard_map/pallas_call | solution.py:423
  58.6 0.0 copy-start
  58.6 1.2 %copy.11 = bf16[8,16,2,8,128]{4,3,2,1,0:T(8,128)(2,1)S(1)} copy(bf16[8,16,2,8,128]{4,3,0,2,1:T(8,128)(2,1)} %bitcast.10) | data formatting | bytes 1048576 | tf_op jit(solution)/shard_map/transpose | solution.py:484
  59.8 0.2 reshape.11
  60.0 0.0 copy-done
  60.0 0.9 %select_bitcast_fusion = bf16[1,128,2048]{2,1,0:T(8,128)(2,1)} fusion(bf16[128,2048]{1,0:T(8,128)(2,1)S(1)} %copy-done, bf16[128,2048]{1,0:T(8,128)(2,1)S(1)} %reshape.11, pred[]{:T(512)S(6)} %eq.3), kind=kLoop, calls=%fused_computation | loop fusion | flops 262144 | bytes 1572865 | tf_op jit(solution)/shard_map/broadcast_in_dim | solution.py:486
Async XLA Ops:
  58.6 1.4 %copy-start = (bf16[128,2048]{1,0:T(8,128)(2,1)S(1)}, bf16[128,2048]{1,0:T(8,128)(2,1)}, u32[]{:S(2)}) copy-start(bf16[128,2048]{1,0:T(8,128)(2,1)} %get-tuple-element.7) | copy-start | bytes 1572868

commit v9 on v8

--- a/solution.py
+++ b/solution.py
@@ -80,7 +80,7 @@
     slabs, ogs, master_v, moment1_v, moment2_v, fresh, sums, parts, slots, reduced, val_slots,
     og_send, og_recv, hid_send, hid_recv, loc, x_send, x_recv, c_send, c_recv,
     p_send, p_recv, b_send, b_recv, v_send, v_recv,
-    vals, queries_v, asked_v, keys_v, k_v, v_v, cache_out, fresh_wts, att_sem,
+    vals, queries_v, asked_v, keys_v, k_v, v_v, cache_out, fresh_wts, placed_out, placed_wts, att_sem,
 ):
     r, i, t = position()
     q = n // m
@@ -191,15 +191,25 @@
             fresh_exp = jnp.exp(fresh_score - top)
             total = jnp.sum(cache_exp, axis=-1, keepdims=True) + jnp.sum(fresh_exp, axis=-1, keepdims=True)
             cache_wts = (cache_exp / total).astype(jnp.bfloat16)
-            fresh_wts[row, k] = (fresh_exp / total).astype(jnp.bfloat16)
+            fresh_wts[row, k] = fresh_exp / total
             cache_out[row, k] = jnp.dot(cache_wts, v_v[row, :, at], preferred_element_type=jnp.float32)
 
-    def finish_row(row):
+    def place_rows():
+        for s in range(STEPS):
+            at = slice(s * replica_rows, (s + 1) * replica_rows)
+            for k in range(kv_heads):
+                for h in range(share):
+                    head = k * share + h
+                    placed_out[at, head * HD : (head + 1) * HD] = cache_out[:, k, s * share + h, :]
+                    placed_wts[head, at, :] = fresh_wts[:, k, s * share + h, :].astype(jnp.bfloat16)
+
+    def finish():
         for k in range(kv_heads):
-            new = jnp.dot(
-                fresh_wts[row, k], vals[:, k * HD : (k + 1) * HD], preferred_element_type=jnp.float32
-            )
-            att[row, k] = (cache_out[row, k] + new).astype(att.dtype)
+            new_values = vals[:, k * HD : (k + 1) * HD]
+            for head in range(k * share, (k + 1) * share):
+                at = slice(head * HD, (head + 1) * HD)
+                new = jnp.dot(placed_wts[head], new_values, preferred_element_type=jnp.float32)
+                att[:, at] = (placed_out[:, at] + new).astype(att.dtype)
 
     drain(ogs.at[pl.ds(0, n - 1)], og_recv)
     og_local.wait()
@@ -292,6 +302,7 @@
     @pl.when(r == 1)
     def _():
         each(replica_rows - half_rows, lambda k: attend_row(half_rows + k))
+        place_rows()
 
     def send_sum(j):
         slot = r * n + i if split else i
@@ -383,7 +394,7 @@
         drain(val_slots.at[pl.ds(0, sources - 1)], v_recv)
         kept.wait()
         total_of(val_slots, sources, vals, 16)
-        each(replica_rows, finish_row)
+        finish()
         drain(val_slots.at[pl.ds(0, n - 1)], v_send)
         drain(reduced, b_send)
 
@@ -424,7 +435,7 @@
         functools.partial(fused_kernel, n, m, split),
         out_shape=(
             jax.ShapeDtypeStruct((tokens, q * full), jnp.bfloat16),
-            jax.ShapeDtypeStruct(asked, jnp.bfloat16),
+            jax.ShapeDtypeStruct((tokens, queries.shape[2]), jnp.bfloat16),
         ),
         in_specs=[anywhere] * 9 + [pl.BlockSpec(memory_space=pltpu.SMEM)],
         out_specs=(anywhere, pl.BlockSpec(memory_space=pltpu.VMEM)),
@@ -450,7 +461,9 @@
             pltpu.VMEM(k_cache.shape, k_cache.dtype),
             pltpu.VMEM(v_cache.shape, v_cache.dtype),
             pltpu.VMEM(asked, jnp.float32),
-            pltpu.VMEM(asked[:3] + (tokens,), jnp.bfloat16),
+            pltpu.VMEM(asked[:3] + (tokens,), jnp.float32),
+            pltpu.VMEM((tokens, queries.shape[2]), jnp.float32),
+            pltpu.VMEM((queries.shape[2] // HD, tokens, tokens), jnp.bfloat16),
             dma((4,)),
         ],
         compiler_params=pltpu.CompilerParams(
@@ -466,7 +479,6 @@
     n, m = lax.axis_size("dp"), lax.axis_size("tp")
     replica_rows = cache_len.shape[0]
     heads_here = out_grad.shape[1] // HD
-    share = QH // KVH
     learner_rows, attended = fused(
         hidden[0],
         out_grad,
@@ -481,8 +493,7 @@
         n,
         m,
     )
-    decoded = attended.reshape(replica_rows, heads_here, STEPS, share, HD).transpose(2, 0, 1, 3, 4)
-    result = jnp.where(is_learner, learner_rows, decoded.reshape(learner_rows.shape))
+    result = jnp.where(is_learner, learner_rows, attended)
     return result[None]
 
 

time: 61 us -> 60.6 us (level)
  local copies, waits for them, and re-layouts: 1.42 us -> 0 us
  other arithmetic: 0.85 us -> 1.9 us
    transpose x1 -> x0, local copies, waits for them, and re-layouts: 1.19 us -> none  [local(): attended.reshape(replica_rows, heads_here, STEPS, share, HD)]
    broadcast_in_dim x1, other arithmetic: 0.85 us -> 1.9 us  [local(): return result[None]]
where the time goes in v9:
time: 60.6 us; the launch traced here: 60.5 us
  Pallas kernels  58.6 us (97%)
  other arithmetic  1.9 us (3%)
    pallas_call x1, Pallas kernels, fused(): pl.pallas_call(functools.partial(fused_kernel, n, m, split), out_shape=(j...  58.6 us
    broadcast_in_dim x1, other arithmetic, local(): return result[None]  1.9 us

profile of v9, /device:TPU:2, one launch (start us, length us, event | category | flops | bytes accessed | tf_op | source)
XLA Modules:
  0.0 60.5 jit_solution(14847675370112990136)
XLA Ops:
  0.0 58.6 %shard_map.100 = (bf16[128,2048]{1,0:T(8,128)(2,1)}, bf16[128,2048]{1,0:T(8,128)(2,1)}) custom-call(bf16[128,8192]{1,0:T(8,128)(2,1)} %bitcast.4, bf16[128,256]{1,0:T(8,128)(2,1)} %og.1, f32[2048,256]{1,0:T(8,128)} %master.1, f32[2048,256]{1,0:T(8,128)} %moment1.1, f32[2048,256]{1,0:T(8,128)} %moment2.1, bf16[8,16,2048]{2,1,0:T(8,128)(2,1)} %queries.1, ...), custom_call_target="tpu_custom_call" | custom-call | tf_op jit(solution)/shard_map/pallas_call | solution.py:434
  58.6 1.9 %select_bitcast_fusion = bf16[1,128,2048]{2,1,0:T(8,128)(2,1)} fusion(bf16[128,2048]{1,0:T(8,128)(2,1)} %get-tuple-element.7, bf16[128,2048]{1,0:T(8,128)(2,1)} %get-tuple-element.8, pred[]{:T(512)S(6)} %eq.3), kind=kLoop, calls=%fused_computation | loop fusion | flops 262144 | bytes 1572865 | tf_op jit(solution)/shard_map/broadcast_in_dim | solution.py:497
